TPU v7x, 512 devices: a whole 4x4x16 slice. The times are simulated.
512 devices in a mesh: frame: 16 (over x, y), head: 16 (over z), tok: 2 (over core).
Axes of the slice: x: 4, y: 4, z: 16, core: 2. Of those that a mesh axis runs over, the one named last changes fastest.
Arguments:
- queries: bfloat16 [16, 3072, 2048], P('frame', ('head', 'tok')), may hold values from -120 to 120
- keys: bfloat16 [16, 3072, 2048], P('frame', ('head', 'tok')), may hold values from -4 to 4
- values: bfloat16 [16, 3072, 2048], P('frame', ('head', 'tok')), may hold values from -6 to 6
- residual: bfloat16 [16, 3072, 2048], P('frame', ('head', 'tok')), may hold values from -6 to 6
- incoming: bfloat16 [3072, 2048], P(('head', 'tok')), may hold values from -6 to 6
- gate_table: float32 [50, 2048], replicated, may hold values from -2 to 2
- timesteps: int32 [16], P('frame'), may hold values from 0 to 49
- positions: int32 [16], P('frame'), may hold values from 0 to 45, as said below
Outputs:
- next_queue: bfloat16 [16, 3072, 2048], P('frame', ('head', 'tok'))
- leaving: bfloat16 [3072, 2048], P(('head', 'tok'), 'frame')
Inputs may be any that keep to these rules, and one draw needn't show every extreme that they name: positions rise strictly along the queue, by 1 to 5 from one frame to the next; the first frame's position is 0 and the last frame's is 45.
All inputs are finite; a program needn't handle non-finite values.
Results may differ from a plain program's by a relative error of at most 0.007.
Values may be sent and summed in bfloat16 or wider, within the bound.
No kernel may reach another device: no remote copies, remote signals or barrier semaphores. Data moves between devices by JAX's collectives and lax.ppermute only.
A program may use at most 64 MiB of HBM per device.

v0:
```python
import functools
import math

import jax
import jax.numpy as jnp
from jax import lax
from jax.experimental import pallas as pl
from jax.experimental.pallas import tpu as pltpu
from jax.sharding import PartitionSpec as P

HD = 128
ROPE_DIMS = 16
EXP2_SCALE = math.log2(math.e) / math.sqrt(HD)
VMEM = pl.BlockSpec(memory_space=pltpu.VMEM)
SMEM = pl.BlockSpec(memory_space=pltpu.SMEM)


def shifted(block, axis, distance):
    devices = range(lax.axis_size(axis))
    route = [(i - distance, i) for i in devices if i - distance in devices]
    return lax.ppermute(block, axis, route)


def swapped(block):
    return lax.ppermute(block, "tok", [(0, 1), (1, 0)])


def pack_kernel(position_ref, q_ref, k_ref, v_ref, out_ref):
    tokens = q_ref.shape[1]
    half = ROPE_DIMS // 2
    lane = lax.broadcasted_iota(jnp.int32, (8, HD), 1)
    pair = jnp.where(lane < half, lane, lane - half)
    angle = position_ref[0].astype(jnp.float32) * jnp.exp2(-pair.astype(jnp.float32))
    turns = lane < ROPE_DIMS
    cosine = jnp.where(turns, jnp.cos(angle), 1.0)[:1]
    sine = jnp.sin(angle)
    from_second = jnp.where(lane < half, -sine, 0.0)[:1]
    from_leading = jnp.where(turns & (lane >= half), sine, 0.0)[:1]
    for head in range(out_ref.shape[0]):
        columns = slice(head * HD, (head + 1) * HD)
        for place, ref in enumerate((q_ref, k_ref)):
            x = ref[0, :, columns].astype(jnp.float32)
            turned = (
                x * cosine
                + pltpu.roll(x, HD - half, 1) * from_second
                + pltpu.roll(x, half, 1) * from_leading
            )
            out_ref[head, place * tokens : (place + 1) * tokens, :] = turned.astype(jnp.bfloat16)
        out_ref[head, 2 * tokens : 3 * tokens, :] = v_ref[0, :, columns]


def pack(positions, queries, keys, values):
    _, tokens, columns = queries.shape
    return pl.pallas_call(
        pack_kernel,
        out_shape=jax.ShapeDtypeStruct((columns // HD, 3 * tokens, HD), jnp.bfloat16),
        in_specs=[SMEM, VMEM, VMEM, VMEM],
        out_specs=VMEM,
        compiler_params=pltpu.CompilerParams(vmem_limit_bytes=16 * 2**20),
        name="pack",
    )(positions, queries, keys, values)


def attend_blocks(q_ref, pair_refs, before, after, query_rows, key_rows):
    groups, tokens, _ = q_ref.shape
    query_groups = query_rows // tokens
    key_groups = key_rows // tokens

    def one_block(index, carry):
        rows = pl.ds(pl.multiple_of(index * query_rows, query_rows), query_rows)
        q = q_ref[pl.ds(index * query_groups, query_groups)].reshape(query_rows, HD)
        chunks = [(ref, g) for ref in pair_refs for g in range(0, groups, key_groups)]

        def scores_of(chunk):
            ref, g = chunk
            k = ref[g : g + key_groups, :tokens, :].reshape(key_rows, HD)
            return lax.dot_general(
                q, k, (((1,), (1,)), ((), ())), preferred_element_type=jnp.float32
            )

        if before is None:
            highest = None
        else:
            highest, total, blended = (ref[rows, :] for ref in before)
            highest = highest[:, :1]
        scores = scores_of(chunks[0])
        for place, (ref, g) in enumerate(chunks):
            following = scores_of(chunks[place + 1]) if place + 1 < len(chunks) else None
            summit = jnp.max(scores, axis=1, keepdims=True) * EXP2_SCALE
            if highest is not None:
                summit = jnp.maximum(highest, summit)
            weights = jnp.exp2(scores * EXP2_SCALE - summit).astype(jnp.bfloat16)
            v = ref[g : g + key_groups, tokens:, :].reshape(key_rows, HD)
            both = lax.dot_general(
                weights,
                jnp.concatenate([v, jnp.ones_like(v)], axis=1),
                (((1,), (0,)), ((), ())),
                preferred_element_type=jnp.float32,
            )
            if highest is None:
                blended, total = both[:, :HD], both[:, HD:]
            else:
                factor = jnp.exp2(highest - summit)
                blended = blended * factor + both[:, :HD]
                total = total * factor + both[:, HD:]
            highest = summit
            scores = following
        for ref, result in zip(after, (jnp.broadcast_to(highest, total.shape), total, blended)):
            ref[rows, :] = result
        return carry

    lax.fori_loop(0, groups * tokens // query_rows, one_block, 0)


def own_kernel(q_ref, own_ref, peer_ref, *running, query_rows, key_rows):
    attend_blocks(q_ref, (own_ref, peer_ref), None, running, query_rows, key_rows)


def near_kernel(
    usable_ref, q_ref, highest, total, blended, *refs, query_rows, key_rows
):
    *pairs, out_ref, highest_s, total_s, blended_s = refs
    start = (highest, total, blended)
    running = (highest_s, total_s, blended_s)

    def finish(total, blended):
        out_ref[...] = (
            (blended[...] / total[...]).astype(jnp.bfloat16).reshape(out_ref.shape)
        )

    has_before, has_after = usable_ref[0] > 0, usable_ref[1] > 0

    @pl.when(has_before)
    def _():
        attend_blocks(q_ref, pairs[:2], start, running, query_rows, key_rows)

    @pl.when(jnp.logical_not(has_before))
    def _():
        for ref, given in zip(running, start):
            ref[...] = given[...]

    @pl.when(has_after)
    def _():
        attend_blocks(q_ref, pairs[2:], running, running, query_rows, key_rows)

    finish(total_s, blended_s)


def attention_of(q, own, peer, usable, near, query_rows, key_rows):
    groups, tokens, _ = q.shape
    rows = groups * tokens
    state = jax.ShapeDtypeStruct((rows, HD), jnp.float32)
    params = pltpu.CompilerParams(vmem_limit_bytes=40 * 2**20)
    sizes = dict(query_rows=query_rows, key_rows=key_rows)
    running = pl.pallas_call(
        functools.partial(own_kernel, **sizes),
        out_shape=[state] * 3,
        in_specs=[VMEM] * 3,
        out_specs=[VMEM] * 3,
        compiler_params=params,
        cost_estimate=pl.CostEstimate(
            flops=8 * rows * rows * HD, bytes_accessed=5 * rows * HD * 4, transcendentals=rows * rows
        ),
        name="attend_own",
    )(q, own, peer)
    return pl.pallas_call(
        functools.partial(near_kernel, **sizes),
        out_shape=jax.ShapeDtypeStruct(q.shape, jnp.bfloat16),
        in_specs=[SMEM] + [VMEM] * 8,
        out_specs=VMEM,
        scratch_shapes=[pltpu.VMEM((rows, HD), jnp.float32)] * 3,
        compiler_params=params,
        name="attend_near",
    )(usable, q, *running, *near)


def update_kernel(step_ref, returned_ref, residual_ref, gate_ref, updated_ref, blocks_ref):
    gate = gate_ref[pl.ds(step_ref[0], 1), :]
    for head in range(returned_ref.shape[0]):
        columns = slice(head * HD, (head + 1) * HD)
        updated = (
            residual_ref[0, :, columns].astype(jnp.float32)
            + gate[:, columns] * returned_ref[head].astype(jnp.float32)
        ).astype(jnp.bfloat16)
        updated_ref[0, :, columns] = updated
        blocks_ref[head] = updated


def update(timesteps, returned, residual, gate_table):
    return pl.pallas_call(
        update_kernel,
        out_shape=[
            jax.ShapeDtypeStruct(residual.shape, jnp.bfloat16),
            jax.ShapeDtypeStruct(returned.shape, jnp.bfloat16),
        ],
        in_specs=[SMEM, VMEM, VMEM, VMEM],
        out_specs=[VMEM, VMEM],
        compiler_params=pltpu.CompilerParams(vmem_limit_bytes=16 * 2**20),
        name="update",
    )(timesteps, returned, residual, gate_table)


def per_device(queries, keys, values, residual, incoming, gate_table, timesteps, positions):
    tokens = queries.shape[1]
    frame_index = lax.axis_index("frame")
    last_index = lax.axis_size("frame") - 1
    packed = pack(positions, queries, keys, values)
    received = lax.all_to_all(packed, "head", split_axis=0, concat_axis=0, tiled=True)
    q, own = received[:, :tokens], received[:, tokens:]
    prior = shifted(own, "frame", 1)
    later = shifted(own, "frame", -1)
    peer = swapped(own)
    near = (prior, swapped(prior), later, swapped(later))
    usable = jnp.stack([frame_index > 0, frame_index < last_index]).astype(jnp.int32)
    attention = attention_of(q, own, peer, usable, near, 384, 1536)
    returned = lax.all_to_all(attention, "head", split_axis=0, concat_axis=0, tiled=True)
    updated, blocks = update(timesteps, returned, residual, gate_table)
    arriving = shifted(updated, "frame", -1)
    departed = lax.all_to_all(blocks, "frame", split_axis=0, concat_axis=0, tiled=True)
    next_queue = jnp.where(frame_index == last_index, incoming[None], arriving)
    return (next_queue, departed[0])


def solution(mesh):
    placed = (
        P("frame", ("head", "tok"), None),
        P("frame", ("head", "tok"), None),
        P("frame", ("head", "tok"), None),
        P("frame", ("head", "tok"), None),
        P(("head", "tok"), None),
        P(),
        P("frame"),
        P("frame"),
    )
    return jax.shard_map(
        per_device,
        mesh=mesh,
        in_specs=placed,
        out_specs=(P("frame", ("head", "tok"), None), P(("head", "tok"), "frame")),
        check_vma=False,
    )
```

profile of v0, /device:TPU:56, one launch (start us, length us, event | category | flops | bytes accessed | tf_op | source)
XLA Modules:
  0.0 185.1 jit_solution(11906955394014262773)
XLA Ops:
  1.3 0.0 copy-start.1
  1.3 1.0 copy-done.1
  2.3 1.0 copy-done.2
  3.3 1.0 copy-done.3
  4.3 0.6 pack.1
  4.9 74.1 %all_to_all.15 = bf16[16,288,128]{2,1,0:T(8,128)(2,1)S(1)} all-to-all(bf16[16,288,128]{2,1,0:T(8,128)(2,1)S(1)} %pack.1), channel_id=1, replica_groups=mesh['frame'=16,'head'=16,'tok'=2] {'head'}, dimensions={0} | all-to-all | bytes 2359296 | tf_op jit(solution)/shard_map/all_to_all | solution.py:208
  79.0 1.1 slice.13.own_ref
  80.0 3.0 %collective-permute-start.1 = (bf16[16,192,128]{2,1,0:T(8,128)(2,1)}, bf16[16,192,128]{2,1,0:T(8,128)(2,1)S(1)}, u32[]{:S(2)}, u32[]{:S(2)}) collective-permute-start(bf16[16,192,128]{2,1,0:T(8,128)(2,1)} %slice.13.own_ref), channel_id=1, source_target_pairs={{0,32},{32,64},{64,96},{96,128},{128,160},{160,192},{192,224},{224... | collective-permute-start | bytes 2359304 | tf_op jit(solution)/shard_map/ppermute | solution.py:21
  83.1 2.8 %collective-permute-start.3 = (bf16[16,192,128]{2,1,0:T(8,128)(2,1)}, bf16[16,192,128]{2,1,0:T(8,128)(2,1)S(1)}, u32[]{:S(2)}, u32[]{:S(2)}) collective-permute-start(bf16[16,192,128]{2,1,0:T(8,128)(2,1)} %slice.13.own_ref), channel_id=1, source_target_pairs={{32,0},{64,32},{96,64},{128,96},{160,128},{192,160},{224,192},{256... | collective-permute-start | bytes 2359304 | tf_op jit(solution)/shard_map/ppermute | solution.py:21
  85.9 1.9 %collective-permute-start = (bf16[16,192,128]{2,1,0:T(8,128)(2,1)}, bf16[16,192,128]{2,1,0:T(8,128)(2,1)}, u32[]{:S(2)}, u32[]{:S(2)}) collective-permute-start(bf16[16,192,128]{2,1,0:T(8,128)(2,1)} %slice.13.own_ref), channel_id=1, source_target_pairs={{0,1},{1,0},{2,3},{3,2},{4,5},{5,4},{6,7},{7,6},{8,9},{9,8},{10,11... | collective-permute-start | bytes 2359304 | tf_op jit(solution)/shard_map/ppermute | solution.py:25
  87.8 12.0 %collective-permute-done.1.refs_0_ = bf16[16,192,128]{2,1,0:T(8,128)(2,1)S(1)} collective-permute-done((bf16[16,192,128]{2,1,0:T(8,128)(2,1)}, bf16[16,192,128]{2,1,0:T(8,128)(2,1)S(1)}, u32[]{:S(2)}, u32[]{:S(2)}) %collective-permute-start.1) | collective-permute-done | bytes 786464 | tf_op jit(solution)/shard_map/ppermute | solution.py:21
  99.8 1.9 %collective-permute-start.2 = (bf16[16,192,128]{2,1,0:T(8,128)(2,1)S(1)}, bf16[16,192,128]{2,1,0:T(8,128)(2,1)S(1)}, u32[]{:S(2)}, u32[]{:S(2)}) collective-permute-start(bf16[16,192,128]{2,1,0:T(8,128)(2,1)S(1)} %collective-permute-done.1.refs_0_), channel_id=1, source_target_pairs={{0,1},{1,0},{2,3},{3,2},{4,5},{5,4},{6,7},{7,6},{8,9},{9,8},{10,11... | collective-permute-start | bytes 2359304 | tf_op jit(solution)/shard_map/ppermute | solution.py:25
  101.8 3.0 %collective-permute-done.3.refs_2_ = bf16[16,192,128]{2,1,0:T(8,128)(2,1)S(1)} collective-permute-done((bf16[16,192,128]{2,1,0:T(8,128)(2,1)}, bf16[16,192,128]{2,1,0:T(8,128)(2,1)S(1)}, u32[]{:S(2)}, u32[]{:S(2)}) %collective-permute-start.3) | collective-permute-done | bytes 786464 | tf_op jit(solution)/shard_map/ppermute | solution.py:21
  104.7 1.9 %collective-permute-start.4 = (bf16[16,192,128]{2,1,0:T(8,128)(2,1)S(1)}, bf16[16,192,128]{2,1,0:T(8,128)(2,1)S(1)}, u32[]{:S(2)}, u32[]{:S(2)}) collective-permute-start(bf16[16,192,128]{2,1,0:T(8,128)(2,1)S(1)} %collective-permute-done.3.refs_2_), channel_id=1, source_target_pairs={{0,1},{1,0},{2,3},{3,2},{4,5},{5,4},{6,7},{7,6},{8,9},{9,8},{10,11... | collective-permute-start | bytes 2359304 | tf_op jit(solution)/shard_map/ppermute | solution.py:25
  106.7 0.1 add_convert_fusion.usable_ref
  106.7 1.0 slice.12.q_ref
  107.8 0.0 collective-permute-done.peer_ref
  107.8 7.8 %attend_own.1 = (f32[1536,128]{1,0:T(8,128)S(1)}, f32[1536,128]{1,0:T(8,128)S(1)}, f32[1536,128]{1,0:T(8,128)S(1)}) custom-call(bf16[16,96,128]{2,1,0:T(8,128)(2,1)S(1)} %slice.12.q_ref, bf16[16,192,128]{2,1,0:T(8,128)(2,1)} %slice.13.own_ref, bf16[16,192,128]{2,1,0:T(8,128)(2,1)} %collective-permute-done.peer_ref), custom_call_target="tpu_custom_call" | custom-call | flops 2415919104 | bytes 3932160 | tf_op jit(solution)/shard_map/attend_own/pallas_call | solution.py:155
  115.6 0.0 collective-permute-done.2.refs_1_
  115.6 0.0 collective-permute-done.4.refs_3_
  115.6 0.0 copy-start.4
  115.6 15.9 %attend_near.1 = bf16[16,96,128]{2,1,0:T(8,128)(2,1)} custom-call(s32[2]{0:T(128)S(1)} %add_convert_fusion.usable_ref, bf16[16,96,128]{2,1,0:T(8,128)(2,1)S(1)} %slice.12.q_ref, f32[1536,128]{1,0:T(8,128)S(1)} %get-tuple-element.7.highest, f32[1536,128]{1,0:T(8,128)S(1)} %get-tuple-element.8.total, f32[1536,128]{1,0:T(8,128)S(1)} %get-tuple-element.9.blended, ...), custom_call_target="tpu_custom_call" | custom-call | tf_op jit(solution)/shard_map/attend_near/pallas_call | solution.py:166
  131.5 5.9 %all-to-all-start.1 = ((bf16[16,96,128]{2,1,0:T(8,128)(2,1)}), bf16[16,96,128]{2,1,0:T(8,128)(2,1)S(1)}, u32[]{:S(2)}, u32[]{:S(2)}) async-start(bf16[16,96,128]{2,1,0:T(8,128)(2,1)} %attend_near.1), calls=%async_computation.1 | async-start | bytes 786432 | tf_op jit(solution)/shard_map/all_to_all | solution.py:216
  138.1 21.7 %all-to-all-done.1.returned_ref = bf16[16,96,128]{2,1,0:T(8,128)(2,1)S(1)} async-done(((bf16[16,96,128]{2,1,0:T(8,128)(2,1)}), bf16[16,96,128]{2,1,0:T(8,128)(2,1)S(1)}, u32[]{:S(2)}, u32[]{:S(2)}) %all-to-all-start.1) | async-done | bytes 393248 | tf_op jit(solution)/shard_map/all_to_all | solution.py:216
  159.8 1.0 copy-done
  160.8 0.9 update.1
  161.7 6.7 %all-to-all-start.2 = ((bf16[16,96,128]{2,1,0:T(8,128)(2,1)}), bf16[16,96,128]{2,1,0:T(8,128)(2,1)S(1)}, u32[]{:S(2)}, u32[]{:S(2)}) async-start(bf16[16,96,128]{2,1,0:T(8,128)(2,1)} %get-tuple-element.11), calls=%async_computation.2 | async-start | bytes 786432 | tf_op jit(solution)/shard_map/all_to_all | solution.py:219
  168.4 2.8 %collective-permute-start.5 = (bf16[1,96,2048]{2,1,0:T(8,128)(2,1)S(1)}, bf16[1,96,2048]{2,1,0:T(8,128)(2,1)S(1)}, u32[]{:S(2)}, u32[]{:S(2)}) collective-permute-start(bf16[1,96,2048]{2,1,0:T(8,128)(2,1)S(1)} %get-tuple-element.10), channel_id=1, source_target_pairs={{32,0},{64,32},{96,64},{128,96},{160,128},{192,160},{224,192},{256... | collective-permute-start | bytes 1179656 | tf_op jit(solution)/shard_map/ppermute | solution.py:21
  171.1 5.8 %all-to-all-done.2 = bf16[16,96,128]{2,1,0:T(8,128)(2,1)S(1)} async-done(((bf16[16,96,128]{2,1,0:T(8,128)(2,1)}), bf16[16,96,128]{2,1,0:T(8,128)(2,1)S(1)}, u32[]{:S(2)}, u32[]{:S(2)}) %all-to-all-start.2) | async-done | bytes 393248 | tf_op jit(solution)/shard_map/all_to_all | solution.py:219
  176.9 0.6 slice_bitcast_fusion
  177.5 6.8 %collective-permute-done.5 = bf16[1,96,2048]{2,1,0:T(8,128)(2,1)S(1)} collective-permute-done((bf16[1,96,2048]{2,1,0:T(8,128)(2,1)S(1)}, bf16[1,96,2048]{2,1,0:T(8,128)(2,1)S(1)}, u32[]{:S(2)}, u32[]{:S(2)}) %collective-permute-start.5) | collective-permute-done | bytes 393248 | tf_op jit(solution)/shard_map/ppermute | solution.py:21
  184.3 0.8 bitcast_select_fusion
  (8 shorter events, 0.0 us)
Async XLA Ops:
  1.3 1.0 copy-start.1
  2.3 1.0 copy-start.2
  3.3 1.0 copy-start.3
  79.0 25.8 %copy-start.5 = (bf16[16,288,128]{2,1,0:T(8,128)(2,1)}, bf16[16,288,128]{2,1,0:T(8,128)(2,1)S(1)}, u32[]{:S(2)}) copy-start(bf16[16,288,128]{2,1,0:T(8,128)(2,1)S(1)} %all_to_all.15) | copy-start | bytes 3538948
  80.0 19.8 %collective-permute-start.1 = (bf16[16,192,128]{2,1,0:T(8,128)(2,1)}, bf16[16,192,128]{2,1,0:T(8,128)(2,1)S(1)}, u32[]{:S(2)}, u32[]{:S(2)}) collective-permute-start(bf16[16,192,128]{2,1,0:T(8,128)(2,1)} %slice.13.own_ref), channel_id=1, source_target_pairs={{0,32},{32,64},{64,96},{96,128},{128,160},{160,192},{192,224},{224... | collective-permute-start | bytes 2359304 | tf_op jit(solution)/shard_map/ppermute | solution.py:21
  83.1 21.7 %collective-permute-start.3 = (bf16[16,192,128]{2,1,0:T(8,128)(2,1)}, bf16[16,192,128]{2,1,0:T(8,128)(2,1)S(1)}, u32[]{:S(2)}, u32[]{:S(2)}) collective-permute-start(bf16[16,192,128]{2,1,0:T(8,128)(2,1)} %slice.13.own_ref), channel_id=1, source_target_pairs={{32,0},{64,32},{96,64},{128,96},{160,128},{192,160},{224,192},{256... | collective-permute-start | bytes 2359304 | tf_op jit(solution)/shard_map/ppermute | solution.py:21
  85.9 21.9 %collective-permute-start = (bf16[16,192,128]{2,1,0:T(8,128)(2,1)}, bf16[16,192,128]{2,1,0:T(8,128)(2,1)}, u32[]{:S(2)}, u32[]{:S(2)}) collective-permute-start(bf16[16,192,128]{2,1,0:T(8,128)(2,1)} %slice.13.own_ref), channel_id=1, source_target_pairs={{0,1},{1,0},{2,3},{3,2},{4,5},{5,4},{6,7},{7,6},{8,9},{9,8},{10,11... | collective-permute-start | bytes 2359304 | tf_op jit(solution)/shard_map/ppermute | solution.py:25
  99.8 15.7 %collective-permute-start.2 = (bf16[16,192,128]{2,1,0:T(8,128)(2,1)S(1)}, bf16[16,192,128]{2,1,0:T(8,128)(2,1)S(1)}, u32[]{:S(2)}, u32[]{:S(2)}) collective-permute-start(bf16[16,192,128]{2,1,0:T(8,128)(2,1)S(1)} %collective-permute-done.1.refs_0_), channel_id=1, source_target_pairs={{0,1},{1,0},{2,3},{3,2},{4,5},{5,4},{6,7},{7,6},{8,9},{9,8},{10,11... | collective-permute-start | bytes 2359304 | tf_op jit(solution)/shard_map/ppermute | solution.py:25
  104.7 10.8 %collective-permute-start.4 = (bf16[16,192,128]{2,1,0:T(8,128)(2,1)S(1)}, bf16[16,192,128]{2,1,0:T(8,128)(2,1)S(1)}, u32[]{:S(2)}, u32[]{:S(2)}) collective-permute-start(bf16[16,192,128]{2,1,0:T(8,128)(2,1)S(1)} %collective-permute-done.3.refs_2_), channel_id=1, source_target_pairs={{0,1},{1,0},{2,3},{3,2},{4,5},{5,4},{6,7},{7,6},{8,9},{9,8},{10,11... | collective-permute-start | bytes 2359304 | tf_op jit(solution)/shard_map/ppermute | solution.py:25
  115.6 44.2 %copy-start.4 = (bf16[1,96,2048]{2,1,0:T(8,128)(2,1)S(1)}, bf16[1,96,2048]{2,1,0:T(8,128)(2,1)}, u32[]{:S(2)}) copy-start(bf16[1,96,2048]{2,1,0:T(8,128)(2,1)} %residual_ref.1) | copy-start | bytes 1179652
  131.5 52.8 %copy-start.6 = (bf16[96,2048]{1,0:T(8,128)(2,1)S(1)}, bf16[96,2048]{1,0:T(8,128)(2,1)}, u32[]{:S(2)}) copy-start(bf16[96,2048]{1,0:T(8,128)(2,1)} %param.12) | copy-start | bytes 1179652
  131.5 28.2 %all-to-all-start.1 = ((bf16[16,96,128]{2,1,0:T(8,128)(2,1)}), bf16[16,96,128]{2,1,0:T(8,128)(2,1)S(1)}, u32[]{:S(2)}, u32[]{:S(2)}) async-start(bf16[16,96,128]{2,1,0:T(8,128)(2,1)} %attend_near.1), calls=%async_computation.1 | async-start | bytes 786432 | tf_op jit(solution)/shard_map/all_to_all | solution.py:216
  159.8 1.0 copy-start
  161.7 15.2 %all-to-all-start.2 = ((bf16[16,96,128]{2,1,0:T(8,128)(2,1)}), bf16[16,96,128]{2,1,0:T(8,128)(2,1)S(1)}, u32[]{:S(2)}, u32[]{:S(2)}) async-start(bf16[16,96,128]{2,1,0:T(8,128)(2,1)} %get-tuple-element.11), calls=%async_computation.2 | async-start | bytes 786432 | tf_op jit(solution)/shard_map/all_to_all | solution.py:219
  168.4 16.0 %collective-permute-start.5 = (bf16[1,96,2048]{2,1,0:T(8,128)(2,1)S(1)}, bf16[1,96,2048]{2,1,0:T(8,128)(2,1)S(1)}, u32[]{:S(2)}, u32[]{:S(2)}) collective-permute-start(bf16[1,96,2048]{2,1,0:T(8,128)(2,1)S(1)} %get-tuple-element.10), channel_id=1, source_target_pairs={{32,0},{64,32},{96,64},{128,96},{160,128},{192,160},{224,192},{256... | collective-permute-start | bytes 1179656 | tf_op jit(solution)/shard_map/ppermute | solution.py:21
where the time goes:
time: 186 us; the launch traced here: 185 us
  blocking collectives  74.1 us (40%)
  waiting for transfers between devices  49.3 us (27%)
  starting transfers between devices  26.9 us (14%)
  Pallas kernels  25.2 us (14%)
  local copies, waits for them, and re-layouts  6.7 us (4%)
  between operations  2.06 us (1%)
    all_to_all x1, blocking collectives, per_device(): lax.all_to_all(packed, 'head', split_axis=0, concat_axis=0, tiled=True)  74.1 us
    ppermute x3, waiting for transfers between devices, shifted(): return lax.ppermute(block, axis, route)  21.9 us
    all_to_all x1, waiting for transfers between devices, per_device(): lax.all_to_all(attention, 'head', split_axis=0, concat_axis=0, tiled=True)  21.7 us
    pallas_call x1, Pallas kernels, attention_of(): pl.pallas_call(functools.partial(near_kernel, **sizes), out_shape=jax.Sha...  15.9 us
    ppermute x3, starting transfers between devices, shifted(): return lax.ppermute(block, axis, route)  8.58 us
    pallas_call x1, Pallas kernels, attention_of(): pl.pallas_call(functools.partial(own_kernel, **sizes), out_shape=[state]...  7.79 us
    all_to_all x1, starting transfers between devices, per_device(): lax.all_to_all(blocks, 'frame', split_axis=0, concat_axis=0, tiled=True)  6.71 us
    all_to_all x1, starting transfers between devices, per_device(): lax.all_to_all(attention, 'head', split_axis=0, concat_axis=0, tiled=True)  5.91 us
  transfers between devices with their start and end apart: 8, of which 5 were waited for; matrix products, arithmetic and copies ran while one was open for 1% of the time, Pallas kernels for 4%

commit v1 on v0

v1 whole, which is shorter than its diff:
```python
import functools
import math

import jax
import jax.numpy as jnp
from jax import lax
from jax.experimental import pallas as pl
from jax.experimental.pallas import tpu as pltpu
from jax.sharding import PartitionSpec as P

HD = 128
ROPE_DIMS = 16
EXP2_SCALE = math.log2(math.e) / math.sqrt(HD)
VMEM = pl.BlockSpec(memory_space=pltpu.VMEM)
SMEM = pl.BlockSpec(memory_space=pltpu.SMEM)


def shifted(block, axis, distance):
    devices = range(lax.axis_size(axis))
    route = [(i - distance, i) for i in devices if i - distance in devices]
    return lax.ppermute(block, axis, route)


def swapped(block):
    return lax.ppermute(block, "tok", [(0, 1), (1, 0)])


def rotation(position):
    half = ROPE_DIMS // 2
    lane = lax.broadcasted_iota(jnp.int32, (8, HD), 1)
    pair = jnp.where(lane < half, lane, lane - half)
    angle = position.astype(jnp.float32) * jnp.exp2(-pair.astype(jnp.float32))
    turns = lane < ROPE_DIMS
    sine = jnp.sin(angle)
    own = jnp.where(turns, jnp.cos(angle), 1.0)[:1]
    ahead = jnp.where(lane < half, -sine, 0.0)[:1]
    behind = jnp.where(turns & (lane >= half), sine, 0.0)[:1]
    return own, ahead, behind


def rotate(x, factors):
    own, ahead, behind = factors
    half = ROPE_DIMS // 2
    x = x.astype(jnp.float32)
    turned = x * own + pltpu.roll(x, HD - half, 1) * ahead + pltpu.roll(x, half, 1) * behind
    return turned.astype(jnp.bfloat16)


def pack_kernel(position_ref, turned_ref, *refs):
    *kept_refs, out_ref = refs
    tokens = turned_ref.shape[1]
    factors = rotation(position_ref[0])
    for head in range(out_ref.shape[0]):
        columns = slice(head * HD, (head + 1) * HD)
        out_ref[head, :tokens, :] = rotate(turned_ref[0, :, columns], factors)
        for kept_ref in kept_refs:
            out_ref[head, tokens:, :] = kept_ref[0, :, columns]


def pack(positions, *arrays):
    _, tokens, columns = arrays[0].shape
    heads = 8
    block = pl.BlockSpec((1, tokens, heads * HD), lambda i: (0, 0, i))
    rows = len(arrays) * tokens
    return pl.pallas_call(
        pack_kernel,
        grid=(columns // HD // heads,),
        out_shape=jax.ShapeDtypeStruct((columns // HD, rows, HD), jnp.bfloat16),
        in_specs=[SMEM] + [block] * len(arrays),
        out_specs=pl.BlockSpec((heads, rows, HD), lambda i: (i, 0, 0)),
        compiler_params=pltpu.CompilerParams(vmem_limit_bytes=60 * 2**20),
        name="pack",
    )(positions, *arrays)


def attend_block(q, pair_refs, key_rows, refs_at_once):
    def scores_of(refs):
        return [
            lax.dot_general(
                q,
                ref[:, : ref.shape[1] // 2, :].reshape(key_rows, HD),
                (((1,), (1,)), ((), ())),
                preferred_element_type=jnp.float32,
            )
            for ref in refs
        ]

    steps = [
        pair_refs[place : place + refs_at_once]
        for place in range(0, len(pair_refs), refs_at_once)
    ]
    scores = scores_of(steps[0])
    for place, refs in enumerate(steps):
        following = scores_of(steps[place + 1]) if place + 1 < len(steps) else None
        summit = functools.reduce(jnp.maximum, scores)
        summit = jnp.max(summit, axis=1, keepdims=True) * EXP2_SCALE
        if place:
            summit = jnp.maximum(highest, summit)
        both = None
        for part, ref in zip(scores, refs):
            weights = jnp.exp2(part * EXP2_SCALE - summit).astype(jnp.bfloat16)
            v = ref[:, ref.shape[1] // 2 :, :].reshape(key_rows, HD)
            product = lax.dot_general(
                weights,
                jnp.concatenate([v, jnp.ones_like(v)], axis=1),
                (((1,), (0,)), ((), ())),
                preferred_element_type=jnp.float32,
            )
            both = product if both is None else both + product
        running = running * jnp.exp2(highest - summit) + both if place else both
        highest = summit
        scores = following
    return (running[:, :HD] / running[:, HD:]).astype(jnp.bfloat16)


def attend_kernel(usable_ref, q_ref, *refs, query_rows):
    *pairs, out_ref = refs
    groups, tokens, _ = q_ref.shape
    query_groups = query_rows // tokens

    def all_blocks(pair_refs):
        def one_block(index, carry):
            block = pl.ds(index * query_groups, query_groups)
            q = q_ref[block].reshape(query_rows, HD)
            found = attend_block(q, pair_refs, groups * tokens, 2)
            out_ref[block] = found.reshape(query_groups, tokens, HD)
            return carry

        lax.fori_loop(0, groups // query_groups, one_block, 0)

    has_before, has_after = usable_ref[0] > 0, usable_ref[1] > 0

    @pl.when(has_before & has_after)
    def _():
        all_blocks(pairs)

    @pl.when(jnp.logical_not(has_before))
    def _():
        all_blocks(pairs[:2] + pairs[4:])

    @pl.when(jnp.logical_not(has_after))
    def _():
        all_blocks(pairs[:4])


def attend(usable, q, pairs, **sizes):
    groups, tokens, _ = q.shape
    rows = groups * tokens
    return pl.pallas_call(
        functools.partial(attend_kernel, **sizes),
        out_shape=jax.ShapeDtypeStruct(q.shape, jnp.bfloat16),
        in_specs=[SMEM] + [VMEM] * (1 + len(pairs)),
        out_specs=VMEM,
        compiler_params=pltpu.CompilerParams(vmem_limit_bytes=40 * 2**20),
        cost_estimate=pl.CostEstimate(
            flops=24 * rows * rows * HD,
            bytes_accessed=28 * rows * HD,
            transcendentals=6 * rows * rows,
        ),
        name="attend",
    )(usable, q, *pairs)


def update_kernel(
    step_ref, first_ref, returned_ref, residual_ref, incoming_ref, gate_ref, moving_ref, *parts
):
    gate = gate_ref[pl.ds(step_ref[0], 1), :]
    heads = parts[0].shape[0]
    first = first_ref[0] > 0
    for head in range(returned_ref.shape[0]):
        columns = slice(head * HD, (head + 1) * HD)
        updated = (
            residual_ref[0, :, columns].astype(jnp.float32)
            + gate[:, columns] * returned_ref[head].astype(jnp.float32)
        ).astype(jnp.bfloat16)
        moving_ref[0, :, columns] = jnp.where(first, incoming_ref[:, columns], updated)
        parts[head // heads][head % heads] = updated


def update(timesteps, first, returned, residual, incoming, gate_table):
    heads, tokens, _ = returned.shape
    part = jax.ShapeDtypeStruct((heads // 4, tokens, HD), jnp.bfloat16)
    moving, *parts = pl.pallas_call(
        update_kernel,
        out_shape=[jax.ShapeDtypeStruct(residual.shape, jnp.bfloat16)] + [part] * 4,
        in_specs=[SMEM, SMEM, VMEM, VMEM, VMEM, VMEM],
        out_specs=[VMEM] * 5,
        compiler_params=pltpu.CompilerParams(vmem_limit_bytes=16 * 2**20),
        name="update",
    )(timesteps, first, returned, residual, incoming, gate_table)
    return moving, parts


def spread(parts, axis):
    size = lax.axis_size(axis)
    step = len(parts)
    index = lax.axis_index(axis)
    firsts = [lax.ppermute(parts[a], axis, [(0, a * step)]) for a in range(1, step)]
    held = jnp.where(index == 0, parts[0], sum(firsts))
    seconds = [
        lax.ppermute(held[b], axis, [(a, a + b) for a in range(0, size, step)])
        for b in range(1, step)
    ]
    return jnp.where(index % step == 0, held[0], sum(seconds))


def per_device(queries, keys, values, residual, incoming, gate_table, timesteps, positions):
    frame_index = lax.axis_index("frame")
    frames = lax.axis_size("frame")
    own = lax.all_to_all(
        pack(positions, keys, values), "head", split_axis=0, concat_axis=0, tiled=True
    )
    own, packed = lax.optimization_barrier((own, pack(positions, queries)))
    prior = shifted(own, "frame", 1)
    later = shifted(own, "frame", -1)
    q = lax.all_to_all(packed, "head", split_axis=0, concat_axis=0, tiled=True)
    pairs = (own, swapped(own), prior, swapped(prior), later, swapped(later))
    usable = jnp.stack([frame_index > 0, frame_index < frames - 1]).astype(jnp.int32)
    attention = attend(usable, q, pairs, query_rows=384)
    returned = lax.all_to_all(attention, "head", split_axis=0, concat_axis=0, tiled=True)
    first = (frame_index == 0).astype(jnp.int32)[None]
    moving, parts = update(timesteps, first, returned, residual, incoming, gate_table)
    next_queue = lax.ppermute(moving, "frame", [(i, (i - 1) % frames) for i in range(frames)])
    return (next_queue, spread(parts, "frame"))


def solution(mesh):
    placed = (
        P("frame", ("head", "tok"), None),
        P("frame", ("head", "tok"), None),
        P("frame", ("head", "tok"), None),
        P("frame", ("head", "tok"), None),
        P(("head", "tok"), None),
        P(),
        P("frame"),
        P("frame"),
    )
    return jax.shard_map(
        per_device,
        mesh=mesh,
        in_specs=placed,
        out_specs=(P("frame", ("head", "tok"), None), P(("head", "tok"), "frame")),
        check_vma=False,
    )
```

time: 186 us -> 164 us (0.88)
  the two profiles are of different devices: /device:TPU:56 before, /device:TPU:8 now
where the time goes in v1:
time: 164 us; the launch traced here: 163 us
  waiting for transfers between devices  80.1 us (49%)
  starting transfers between devices  54.2 us (33%)
  Pallas kernels  23.5 us (14%)
  local copies, waits for them, and re-layouts  2.79 us (2%)
  between operations  2.15 us (1%)
    all_to_all x1, waiting for transfers between devices, per_device(): lax.all_to_all(pack(positions, keys, values), 'head', split_axis=0, conca...  37.3 us
    all_to_all x1, waiting for transfers between devices, per_device(): lax.all_to_all(attention, 'head', split_axis=0, concat_axis=0, tiled=True)  22.6 us
    pallas_call x1, Pallas kernels, attend(): pl.pallas_call(functools.partial(attend_kernel, **sizes), out_shape=jax.S...  19.1 us
    all_to_all x1, starting transfers between devices, per_device(): lax.all_to_all(pack(positions, keys, values), 'head', split_axis=0, conca...  15.2 us
    all_to_all x1, waiting for transfers between devices, per_device(): q = lax.all_to_all(packed, 'head', split_axis=0, concat_axis=0, tiled=True)  14.6 us
    ppermute x1, starting transfers between devices, per_device(): lax.ppermute(moving, 'frame', [(i, (i - 1) % frames) for i in range(frame...  8.52 us
    all_to_all x1, starting transfers between devices, per_device(): q = lax.all_to_all(packed, 'head', split_axis=0, concat_axis=0, tiled=True)  7.32 us
    all_to_all x1, starting transfers between devices, per_device(): lax.all_to_all(attention, 'head', split_axis=0, concat_axis=0, tiled=True)  6.64 us
  transfers between devices with their start and end apart: 15, of which 6 were waited for; matrix products, arithmetic and copies ran while one was open for 0% of the time, Pallas kernels for 1%

profile of v1, /device:TPU:8, one launch (start us, length us, event | category | flops | bytes accessed | tf_op | source)
XLA Modules:
  0.0 163.4 jit_solution(5210650513515418490)
XLA Ops:
  1.3 2.2 %pack.2 = bf16[16,192,128]{2,1,0:T(8,128)(2,1)} custom-call(s32[1]{0:T(128)S(6)} %copy.12.position_ref, bf16[1,96,2048]{2,1,0:T(8,128)(2,1)} %turned_ref.2, bf16[1,96,2048]{2,1,0:T(8,128)(2,1)} %refs_0_.1), custom_call_target="tpu_custom_call" | custom-call | tf_op jit(solution)/shard_map/pack/pallas_call | solution.py:65
  3.5 15.2 %all-to-all-start = ((bf16[16,192,128]{2,1,0:T(8,128)(2,1)}), bf16[16,192,128]{2,1,0:T(8,128)(2,1)S(1)}, u32[]{:S(2)}, u32[]{:S(2)}) async-start(bf16[16,192,128]{2,1,0:T(8,128)(2,1)} %pack.2), calls=%async_computation | async-start | bytes 1572864 | tf_op jit(solution)/shard_map/all_to_all | solution.py:210
  18.7 2.0 %pack.3 = bf16[16,96,128]{2,1,0:T(8,128)(2,1)} custom-call(s32[1]{0:T(128)S(6)} %copy.12.position_ref, bf16[1,96,2048]{2,1,0:T(8,128)(2,1)} %turned_ref.3), custom_call_target="tpu_custom_call" | custom-call | tf_op jit(solution)/shard_map/pack/pallas_call | solution.py:65
  20.7 37.3 %all-to-all-done.refs_0_ = bf16[16,192,128]{2,1,0:T(8,128)(2,1)S(1)} async-done(((bf16[16,192,128]{2,1,0:T(8,128)(2,1)}), bf16[16,192,128]{2,1,0:T(8,128)(2,1)S(1)}, u32[]{:S(2)}, u32[]{:S(2)}) %all-to-all-start) | async-done | bytes 786464 | tf_op jit(solution)/shard_map/all_to_all | solution.py:210
  58.0 2.3 %collective-permute-start.3 = (bf16[16,192,128]{2,1,0:T(8,128)(2,1)S(1)}, bf16[16,192,128]{2,1,0:T(8,128)(2,1)S(1)}, u32[]{:S(2)}, u32[]{:S(2)}) collective-permute-start(bf16[16,192,128]{2,1,0:T(8,128)(2,1)S(1)} %all-to-all-done.refs_0_), channel_id=1, source_target_pairs={{32,0},{64,32},{96,64},{128,96},{160,128},{192,160},{224,192},{256... | collective-permute-start | bytes 2359304 | tf_op jit(solution)/shard_map/ppermute | solution.py:21
  60.3 3.5 %collective-permute-start.1 = (bf16[16,192,128]{2,1,0:T(8,128)(2,1)S(1)}, bf16[16,192,128]{2,1,0:T(8,128)(2,1)S(1)}, u32[]{:S(2)}, u32[]{:S(2)}) collective-permute-start(bf16[16,192,128]{2,1,0:T(8,128)(2,1)S(1)} %all-to-all-done.refs_0_), channel_id=1, source_target_pairs={{0,32},{32,64},{64,96},{96,128},{128,160},{160,192},{192,224},{224... | collective-permute-start | bytes 2359304 | tf_op jit(solution)/shard_map/ppermute | solution.py:21
  63.8 7.3 %all-to-all-start.1 = ((bf16[16,96,128]{2,1,0:T(8,128)(2,1)}), bf16[16,96,128]{2,1,0:T(8,128)(2,1)S(1)}, u32[]{:S(2)}, u32[]{:S(2)}) async-start(bf16[16,96,128]{2,1,0:T(8,128)(2,1)} %pack.3), calls=%async_computation.1 | async-start | bytes 786432 | tf_op jit(solution)/shard_map/all_to_all | solution.py:216
  71.1 1.9 %collective-permute-start = (bf16[16,192,128]{2,1,0:T(8,128)(2,1)S(1)}, bf16[16,192,128]{2,1,0:T(8,128)(2,1)S(1)}, u32[]{:S(2)}, u32[]{:S(2)}) collective-permute-start(bf16[16,192,128]{2,1,0:T(8,128)(2,1)S(1)} %all-to-all-done.refs_0_), channel_id=1, source_target_pairs={{0,1},{1,0},{2,3},{3,2},{4,5},{5,4},{6,7},{7,6},{8,9},{9,8},{10,11... | collective-permute-start | bytes 2359304 | tf_op jit(solution)/shard_map/ppermute | solution.py:25
  73.1 1.0 collective-permute-done.3.refs_4_
  74.0 1.9 %collective-permute-start.4 = (bf16[16,192,128]{2,1,0:T(8,128)(2,1)S(1)}, bf16[16,192,128]{2,1,0:T(8,128)(2,1)}, u32[]{:S(2)}, u32[]{:S(2)}) collective-permute-start(bf16[16,192,128]{2,1,0:T(8,128)(2,1)S(1)} %collective-permute-done.3.refs_4_), channel_id=1, source_target_pairs={{0,1},{1,0},{2,3},{3,2},{4,5},{5,4},{6,7},{7,6},{8,9},{9,8},{10,11... | collective-permute-start | bytes 2359304 | tf_op jit(solution)/shard_map/ppermute | solution.py:25
  76.0 0.2 collective-permute-done.1.refs_2_
  76.1 2.2 %collective-permute-start.2 = (bf16[16,192,128]{2,1,0:T(8,128)(2,1)S(1)}, bf16[16,192,128]{2,1,0:T(8,128)(2,1)}, u32[]{:S(2)}, u32[]{:S(2)}) collective-permute-start(bf16[16,192,128]{2,1,0:T(8,128)(2,1)S(1)} %collective-permute-done.1.refs_2_), channel_id=1, source_target_pairs={{0,1},{1,0},{2,3},{3,2},{4,5},{5,4},{6,7},{7,6},{8,9},{9,8},{10,11... | collective-permute-start | bytes 2359304 | tf_op jit(solution)/shard_map/ppermute | solution.py:25
  78.4 0.1 add_convert_fusion.usable_ref
  78.5 0.0 collective-permute-done.refs_1_
  78.5 0.9 copy-done.3
  79.4 14.6 %all-to-all-done.1.q_ref = bf16[16,96,128]{2,1,0:T(8,128)(2,1)S(1)} async-done(((bf16[16,96,128]{2,1,0:T(8,128)(2,1)}), bf16[16,96,128]{2,1,0:T(8,128)(2,1)S(1)}, u32[]{:S(2)}, u32[]{:S(2)}) %all-to-all-start.1) | async-done | bytes 393248 | tf_op jit(solution)/shard_map/all_to_all | solution.py:216
  94.0 0.0 collective-permute-done.2.refs_3_
  94.0 1.1 copy-done.4
  95.1 19.1 %attend.1 = bf16[16,96,128]{2,1,0:T(8,128)(2,1)} custom-call(s32[2]{0:T(128)S(1)} %add_convert_fusion.usable_ref, bf16[16,96,128]{2,1,0:T(8,128)(2,1)S(1)} %all-to-all-done.1.q_ref, bf16[16,192,128]{2,1,0:T(8,128)(2,1)S(1)} %all-to-all-done.refs_0_, bf16[16,192,128]{2,1,0:T(8,128)(2,1)S(1)} %copy-done.4, ...), custom_call_target="tpu_custom_call" | custom-call | flops 7247757312 | bytes 5505024 | tf_op jit(solution)/shard_map/attend/pallas_call | solution.py:149
  114.2 6.6 %all-to-all-start.2 = ((bf16[16,96,128]{2,1,0:T(8,128)(2,1)}), bf16[16,96,128]{2,1,0:T(8,128)(2,1)S(1)}, u32[]{:S(2)}, u32[]{:S(2)}) async-start(bf16[16,96,128]{2,1,0:T(8,128)(2,1)} %attend.1), calls=%async_computation.2 | async-start | bytes 786432 | tf_op jit(solution)/shard_map/all_to_all | solution.py:220
  121.5 22.6 %all-to-all-done.2.returned_ref = bf16[16,96,128]{2,1,0:T(8,128)(2,1)S(1)} async-done(((bf16[16,96,128]{2,1,0:T(8,128)(2,1)}), bf16[16,96,128]{2,1,0:T(8,128)(2,1)S(1)}, u32[]{:S(2)}, u32[]{:S(2)}) %all-to-all-start.2) | async-done | bytes 393248 | tf_op jit(solution)/shard_map/all_to_all | solution.py:220
  144.1 0.2 update.1
  144.3 0.7 collective-permute-start.6
  145.0 0.7 collective-permute-start.7
  145.7 0.7 collective-permute-start.8
  146.4 8.5 %collective-permute-start.5 = (bf16[1,96,2048]{2,1,0:T(8,128)(2,1)S(1)}, bf16[1,96,2048]{2,1,0:T(8,128)(2,1)S(1)}, u32[]{:S(2)}, u32[]{:S(2)}) collective-permute-start(bf16[1,96,2048]{2,1,0:T(8,128)(2,1)S(1)} %get-tuple-element.11), channel_id=1, source_target_pairs={{0,480},{32,0},{64,32},{96,64},{128,96},{160,128},{192,160},{224,1... | collective-permute-start | bytes 1179656 | tf_op jit(solution)/shard_map/ppermute | solution.py:223
  155.0 0.7 collective-permute-start.10
  155.6 0.7 collective-permute-start.11
  156.3 1.3 collective-permute-start.9
  157.6 4.4 %collective-permute-done.9 = bf16[96,128]{1,0:T(8,128)(2,1)S(1)} collective-permute-done((bf16[96,128]{1,0:T(8,128)(2,1)S(1)}, bf16[96,128]{1,0:T(8,128)(2,1)S(1)}, u32[]{:S(2)}, u32[]{:S(2)}) %collective-permute-start.9) | collective-permute-done | bytes 24608 | tf_op jit(solution)/shard_map/ppermute | solution.py:201
  162.0 0.6 fusion
  162.6 0.7 copy.13
  (17 shorter events, 0.1 us)
Async XLA Ops:
  3.5 54.5 %all-to-all-start = ((bf16[16,192,128]{2,1,0:T(8,128)(2,1)}), bf16[16,192,128]{2,1,0:T(8,128)(2,1)S(1)}, u32[]{:S(2)}, u32[]{:S(2)}) async-start(bf16[16,192,128]{2,1,0:T(8,128)(2,1)} %pack.2), calls=%async_computation | async-start | bytes 1572864 | tf_op jit(solution)/shard_map/all_to_all | solution.py:210
  58.0 16.1 %collective-permute-start.3 = (bf16[16,192,128]{2,1,0:T(8,128)(2,1)S(1)}, bf16[16,192,128]{2,1,0:T(8,128)(2,1)S(1)}, u32[]{:S(2)}, u32[]{:S(2)}) collective-permute-start(bf16[16,192,128]{2,1,0:T(8,128)(2,1)S(1)} %all-to-all-done.refs_0_), channel_id=1, source_target_pairs={{32,0},{64,32},{96,64},{128,96},{160,128},{192,160},{224,192},{256... | collective-permute-start | bytes 2359304 | tf_op jit(solution)/shard_map/ppermute | solution.py:21
  60.3 15.8 %collective-permute-start.1 = (bf16[16,192,128]{2,1,0:T(8,128)(2,1)S(1)}, bf16[16,192,128]{2,1,0:T(8,128)(2,1)S(1)}, u32[]{:S(2)}, u32[]{:S(2)}) collective-permute-start(bf16[16,192,128]{2,1,0:T(8,128)(2,1)S(1)} %all-to-all-done.refs_0_), channel_id=1, source_target_pairs={{0,32},{32,64},{64,96},{96,128},{128,160},{160,192},{192,224},{224... | collective-permute-start | bytes 2359304 | tf_op jit(solution)/shard_map/ppermute | solution.py:21
  63.8 30.1 %all-to-all-start.1 = ((bf16[16,96,128]{2,1,0:T(8,128)(2,1)}), bf16[16,96,128]{2,1,0:T(8,128)(2,1)S(1)}, u32[]{:S(2)}, u32[]{:S(2)}) async-start(bf16[16,96,128]{2,1,0:T(8,128)(2,1)} %pack.3), calls=%async_computation.1 | async-start | bytes 786432 | tf_op jit(solution)/shard_map/all_to_all | solution.py:216
  71.1 7.3 %collective-permute-start = (bf16[16,192,128]{2,1,0:T(8,128)(2,1)S(1)}, bf16[16,192,128]{2,1,0:T(8,128)(2,1)S(1)}, u32[]{:S(2)}, u32[]{:S(2)}) collective-permute-start(bf16[16,192,128]{2,1,0:T(8,128)(2,1)S(1)} %all-to-all-done.refs_0_), channel_id=1, source_target_pairs={{0,1},{1,0},{2,3},{3,2},{4,5},{5,4},{6,7},{7,6},{8,9},{9,8},{10,11... | collective-permute-start | bytes 2359304 | tf_op jit(solution)/shard_map/ppermute | solution.py:25
  74.0 19.9 %collective-permute-start.4 = (bf16[16,192,128]{2,1,0:T(8,128)(2,1)S(1)}, bf16[16,192,128]{2,1,0:T(8,128)(2,1)}, u32[]{:S(2)}, u32[]{:S(2)}) collective-permute-start(bf16[16,192,128]{2,1,0:T(8,128)(2,1)S(1)} %collective-permute-done.3.refs_4_), channel_id=1, source_target_pairs={{0,1},{1,0},{2,3},{3,2},{4,5},{5,4},{6,7},{7,6},{8,9},{9,8},{10,11... | collective-permute-start | bytes 2359304 | tf_op jit(solution)/shard_map/ppermute | solution.py:25
  76.1 17.8 %collective-permute-start.2 = (bf16[16,192,128]{2,1,0:T(8,128)(2,1)S(1)}, bf16[16,192,128]{2,1,0:T(8,128)(2,1)}, u32[]{:S(2)}, u32[]{:S(2)}) collective-permute-start(bf16[16,192,128]{2,1,0:T(8,128)(2,1)S(1)} %collective-permute-done.1.refs_2_), channel_id=1, source_target_pairs={{0,1},{1,0},{2,3},{3,2},{4,5},{5,4},{6,7},{7,6},{8,9},{9,8},{10,11... | collective-permute-start | bytes 2359304 | tf_op jit(solution)/shard_map/ppermute | solution.py:25
  78.5 0.9 copy-start.3
  94.0 1.1 copy-start.4
  95.1 49.0 %copy-start.1 = (bf16[1,96,2048]{2,1,0:T(8,128)(2,1)S(1)}, bf16[1,96,2048]{2,1,0:T(8,128)(2,1)}, u32[]{:S(2)}) copy-start(bf16[1,96,2048]{2,1,0:T(8,128)(2,1)} %residual_ref.1) | copy-start | bytes 1179652
  95.1 49.0 %copy-start.2 = (bf16[96,2048]{1,0:T(8,128)(2,1)S(1)}, bf16[96,2048]{1,0:T(8,128)(2,1)}, u32[]{:S(2)}) copy-start(bf16[96,2048]{1,0:T(8,128)(2,1)} %incoming_ref.1) | copy-start | bytes 1179652
  114.2 29.9 %copy-start = (f32[50,2048]{1,0:T(8,128)S(1)}, f32[50,2048]{1,0:T(8,128)}, u32[]{:S(2)}) copy-start(f32[50,2048]{1,0:T(8,128)} %gate_ref.1) | copy-start | bytes 1228804
  114.2 29.9 %all-to-all-start.2 = ((bf16[16,96,128]{2,1,0:T(8,128)(2,1)}), bf16[16,96,128]{2,1,0:T(8,128)(2,1)S(1)}, u32[]{:S(2)}, u32[]{:S(2)}) async-start(bf16[16,96,128]{2,1,0:T(8,128)(2,1)} %attend.1), calls=%async_computation.2 | async-start | bytes 786432 | tf_op jit(solution)/shard_map/all_to_all | solution.py:220
  144.3 10.6 %collective-permute-start.6 = (bf16[4,96,128]{2,1,0:T(8,128)(2,1)S(1)}, bf16[4,96,128]{2,1,0:T(8,128)(2,1)S(1)}, u32[]{:S(2)}, u32[]{:S(2)}) collective-permute-start(bf16[4,96,128]{2,1,0:T(8,128)(2,1)S(1)} %get-tuple-element.13), channel_id=1, source_target_pairs={{0,128},{1,129},{2,130},{3,131},{4,132},{5,133},{6,134},{7,135},{8... | collective-permute-start | bytes 294920 | tf_op jit(solution)/shard_map/ppermute | solution.py:198
  145.0 9.9 %collective-permute-start.7 = (bf16[4,96,128]{2,1,0:T(8,128)(2,1)S(1)}, bf16[4,96,128]{2,1,0:T(8,128)(2,1)S(1)}, u32[]{:S(2)}, u32[]{:S(2)}) collective-permute-start(bf16[4,96,128]{2,1,0:T(8,128)(2,1)S(1)} %get-tuple-element.14), channel_id=1, source_target_pairs={{0,256},{1,257},{2,258},{3,259},{4,260},{5,261},{6,262},{7,263},{8... | collective-permute-start | bytes 294920 | tf_op jit(solution)/shard_map/ppermute | solution.py:198
  145.7 9.2 %collective-permute-start.8 = (bf16[4,96,128]{2,1,0:T(8,128)(2,1)S(1)}, bf16[4,96,128]{2,1,0:T(8,128)(2,1)S(1)}, u32[]{:S(2)}, u32[]{:S(2)}) collective-permute-start(bf16[4,96,128]{2,1,0:T(8,128)(2,1)S(1)} %get-tuple-element.15), channel_id=1, source_target_pairs={{0,384},{1,385},{2,386},{3,387},{4,388},{5,389},{6,390},{7,391},{8... | collective-permute-start | bytes 294920 | tf_op jit(solution)/shard_map/ppermute | solution.py:198
  146.4 16.3 %collective-permute-start.5 = (bf16[1,96,2048]{2,1,0:T(8,128)(2,1)S(1)}, bf16[1,96,2048]{2,1,0:T(8,128)(2,1)S(1)}, u32[]{:S(2)}, u32[]{:S(2)}) collective-permute-start(bf16[1,96,2048]{2,1,0:T(8,128)(2,1)S(1)} %get-tuple-element.11), channel_id=1, source_target_pairs={{0,480},{32,0},{64,32},{96,64},{128,96},{160,128},{192,160},{224,1... | collective-permute-start | bytes 1179656 | tf_op jit(solution)/shard_map/ppermute | solution.py:223
  155.0 2.7 %collective-permute-start.10 = (bf16[96,128]{1,0:T(8,128)(2,1)S(1)}, bf16[96,128]{1,0:T(8,128)(2,1)S(1)}, u32[]{:S(2)}, u32[]{:S(2)}) collective-permute-start(bf16[96,128]{1,0:T(8,128)(2,1)S(1)} %get-tuple-element.16), channel_id=1, source_target_pairs={{0,64},{128,192},{256,320},{384,448},{1,65},{129,193},{257,321},{3... | collective-permute-start | bytes 73736 | tf_op jit(solution)/shard_map/ppermute | solution.py:201
  155.6 2.0 %collective-permute-start.11 = (bf16[96,128]{1,0:T(8,128)(2,1)S(1)}, bf16[96,128]{1,0:T(8,128)(2,1)S(1)}, u32[]{:S(2)}, u32[]{:S(2)}) collective-permute-start(bf16[96,128]{1,0:T(8,128)(2,1)S(1)} %get-tuple-element.17), channel_id=1, source_target_pairs={{0,96},{128,224},{256,352},{384,480},{1,97},{129,225},{257,353},{3... | collective-permute-start | bytes 73736 | tf_op jit(solution)/shard_map/ppermute | solution.py:201
  156.3 5.7 %collective-permute-start.9 = (bf16[96,128]{1,0:T(8,128)(2,1)S(1)}, bf16[96,128]{1,0:T(8,128)(2,1)S(1)}, u32[]{:S(2)}, u32[]{:S(2)}) collective-permute-start(bf16[96,128]{1,0:T(8,128)(2,1)S(1)} %get-tuple-element.18), channel_id=1, source_target_pairs={{0,32},{128,160},{256,288},{384,416},{1,33},{129,161},{257,289},{3... | collective-permute-start | bytes 73736 | tf_op jit(solution)/shard_map/ppermute | solution.py:201

commit v2 on v1

--- a/solution.py
+++ b/solution.py
@@ -151,7 +151,7 @@
         out_shape=jax.ShapeDtypeStruct(q.shape, jnp.bfloat16),
         in_specs=[SMEM] + [VMEM] * (1 + len(pairs)),
         out_specs=VMEM,
-        compiler_params=pltpu.CompilerParams(vmem_limit_bytes=40 * 2**20),
+        compiler_params=pltpu.CompilerParams(vmem_limit_bytes=26 * 2**20),
         cost_estimate=pl.CostEstimate(
             flops=24 * rows * rows * HD,
             bytes_accessed=28 * rows * HD,
@@ -191,6 +191,27 @@
     return moving, parts
 
 
+def finish_kernel(leads_ref, moved_ref, own_ref, *refs):
+    *others, next_ref, leaving_ref = refs
+    next_ref[...] = moved_ref[...]
+    passed = sum(ref[...].astype(jnp.float32) for ref in others).astype(jnp.bfloat16)
+    leaving_ref[...] = jnp.where(leads_ref[0] > 0, own_ref[...], passed)
+
+
+def finish(leads, moved, own, others):
+    return pl.pallas_call(
+        finish_kernel,
+        out_shape=[
+            jax.ShapeDtypeStruct(moved.shape, moved.dtype),
+            jax.ShapeDtypeStruct(own.shape, own.dtype),
+        ],
+        in_specs=[SMEM] + [VMEM] * (2 + len(others)),
+        out_specs=[VMEM, VMEM],
+        compiler_params=pltpu.CompilerParams(vmem_limit_bytes=16 * 2**20),
+        name="finish",
+    )(leads, moved, own, *others)
+
+
 def spread(parts, axis):
     size = lax.axis_size(axis)
     step = len(parts)
@@ -201,7 +222,7 @@
         lax.ppermute(held[b], axis, [(a, a + b) for a in range(0, size, step)])
         for b in range(1, step)
     ]
-    return jnp.where(index % step == 0, held[0], sum(seconds))
+    return held[0], seconds
 
 
 def per_device(queries, keys, values, residual, incoming, gate_table, timesteps, positions):
@@ -221,7 +242,9 @@
     first = (frame_index == 0).astype(jnp.int32)[None]
     moving, parts = update(timesteps, first, returned, residual, incoming, gate_table)
     next_queue = lax.ppermute(moving, "frame", [(i, (i - 1) % frames) for i in range(frames)])
-    return (next_queue, spread(parts, "frame"))
+    held, sent = spread(parts, "frame")
+    leads = (frame_index % len(parts) == 0).astype(jnp.int32)[None]
+    return tuple(finish(leads, next_queue, held, sent))
 
 
 def solution(mesh):

time: 164 us -> 164 us (level)
  no operation moved by 1% of the time
where the time goes in v2:
time: 164 us; the launch traced here: 163 us
  waiting for transfers between devices  80.1 us (49%)
  starting transfers between devices  54.2 us (33%)
  Pallas kernels  24.3 us (15%)
  between operations  2.15 us (1%)
  local copies, waits for them, and re-layouts  2.04 us (1%)
    all_to_all x1, waiting for transfers between devices, per_device(): lax.all_to_all(pack(positions, keys, values), 'head', split_axis=0, conca...  37.3 us
    all_to_all x1, waiting for transfers between devices, per_device(): lax.all_to_all(attention, 'head', split_axis=0, concat_axis=0, tiled=True)  22.6 us
    pallas_call x1, Pallas kernels, attend(): pl.pallas_call(functools.partial(attend_kernel, **sizes), out_shape=jax.S...  19.1 us
    all_to_all x1, starting transfers between devices, per_device(): lax.all_to_all(pack(positions, keys, values), 'head', split_axis=0, conca...  15.2 us
    all_to_all x1, waiting for transfers between devices, per_device(): q = lax.all_to_all(packed, 'head', split_axis=0, concat_axis=0, tiled=True)  14.6 us
    ppermute x1, starting transfers between devices, per_device(): lax.ppermute(moving, 'frame', [(i, (i - 1) % frames) for i in range(frame...  8.52 us
    all_to_all x1, starting transfers between devices, per_device(): q = lax.all_to_all(packed, 'head', split_axis=0, concat_axis=0, tiled=True)  7.32 us
    all_to_all x1, starting transfers between devices, per_device(): lax.all_to_all(attention, 'head', split_axis=0, concat_axis=0, tiled=True)  6.64 us
  transfers between devices with their start and end apart: 15, of which 6 were waited for; matrix products, arithmetic and copies ran while one was open for 0% of the time, Pallas kernels for 1%

profile of v2, /device:TPU:8, one launch (start us, length us, event | category | flops | bytes accessed | tf_op | source)
XLA Modules:
  0.0 162.8 jit_solution(6289597074467099530)
XLA Ops:
  1.3 2.2 %pack.2 = bf16[16,192,128]{2,1,0:T(8,128)(2,1)} custom-call(s32[1]{0:T(128)S(6)} %copy.11.position_ref, bf16[1,96,2048]{2,1,0:T(8,128)(2,1)} %turned_ref.2, bf16[1,96,2048]{2,1,0:T(8,128)(2,1)} %refs_0_.1), custom_call_target="tpu_custom_call" | custom-call | tf_op jit(solution)/shard_map/pack/pallas_call | solution.py:65
  3.5 15.2 %all-to-all-start = ((bf16[16,192,128]{2,1,0:T(8,128)(2,1)}), bf16[16,192,128]{2,1,0:T(8,128)(2,1)S(1)}, u32[]{:S(2)}, u32[]{:S(2)}) async-start(bf16[16,192,128]{2,1,0:T(8,128)(2,1)} %pack.2), calls=%async_computation | async-start | bytes 1572864 | tf_op jit(solution)/shard_map/all_to_all | solution.py:231
  18.7 2.0 %pack.3 = bf16[16,96,128]{2,1,0:T(8,128)(2,1)} custom-call(s32[1]{0:T(128)S(6)} %copy.11.position_ref, bf16[1,96,2048]{2,1,0:T(8,128)(2,1)} %turned_ref.3), custom_call_target="tpu_custom_call" | custom-call | tf_op jit(solution)/shard_map/pack/pallas_call | solution.py:65
  20.7 37.3 %all-to-all-done.refs_0_ = bf16[16,192,128]{2,1,0:T(8,128)(2,1)S(1)} async-done(((bf16[16,192,128]{2,1,0:T(8,128)(2,1)}), bf16[16,192,128]{2,1,0:T(8,128)(2,1)S(1)}, u32[]{:S(2)}, u32[]{:S(2)}) %all-to-all-start) | async-done | bytes 786464 | tf_op jit(solution)/shard_map/all_to_all | solution.py:231
  58.0 2.3 %collective-permute-start.3 = (bf16[16,192,128]{2,1,0:T(8,128)(2,1)S(1)}, bf16[16,192,128]{2,1,0:T(8,128)(2,1)S(1)}, u32[]{:S(2)}, u32[]{:S(2)}) collective-permute-start(bf16[16,192,128]{2,1,0:T(8,128)(2,1)S(1)} %all-to-all-done.refs_0_), channel_id=1, source_target_pairs={{32,0},{64,32},{96,64},{128,96},{160,128},{192,160},{224,192},{256... | collective-permute-start | bytes 2359304 | tf_op jit(solution)/shard_map/ppermute | solution.py:21
  60.3 3.5 %collective-permute-start.1 = (bf16[16,192,128]{2,1,0:T(8,128)(2,1)S(1)}, bf16[16,192,128]{2,1,0:T(8,128)(2,1)S(1)}, u32[]{:S(2)}, u32[]{:S(2)}) collective-permute-start(bf16[16,192,128]{2,1,0:T(8,128)(2,1)S(1)} %all-to-all-done.refs_0_), channel_id=1, source_target_pairs={{0,32},{32,64},{64,96},{96,128},{128,160},{160,192},{192,224},{224... | collective-permute-start | bytes 2359304 | tf_op jit(solution)/shard_map/ppermute | solution.py:21
  63.8 7.3 %all-to-all-start.1 = ((bf16[16,96,128]{2,1,0:T(8,128)(2,1)}), bf16[16,96,128]{2,1,0:T(8,128)(2,1)S(1)}, u32[]{:S(2)}, u32[]{:S(2)}) async-start(bf16[16,96,128]{2,1,0:T(8,128)(2,1)} %pack.3), calls=%async_computation.1 | async-start | bytes 786432 | tf_op jit(solution)/shard_map/all_to_all | solution.py:237
  71.1 1.9 %collective-permute-start = (bf16[16,192,128]{2,1,0:T(8,128)(2,1)S(1)}, bf16[16,192,128]{2,1,0:T(8,128)(2,1)S(1)}, u32[]{:S(2)}, u32[]{:S(2)}) collective-permute-start(bf16[16,192,128]{2,1,0:T(8,128)(2,1)S(1)} %all-to-all-done.refs_0_), channel_id=1, source_target_pairs={{0,1},{1,0},{2,3},{3,2},{4,5},{5,4},{6,7},{7,6},{8,9},{9,8},{10,11... | collective-permute-start | bytes 2359304 | tf_op jit(solution)/shard_map/ppermute | solution.py:25
  73.1 1.0 collective-permute-done.3.refs_4_
  74.0 1.9 %collective-permute-start.4 = (bf16[16,192,128]{2,1,0:T(8,128)(2,1)S(1)}, bf16[16,192,128]{2,1,0:T(8,128)(2,1)}, u32[]{:S(2)}, u32[]{:S(2)}) collective-permute-start(bf16[16,192,128]{2,1,0:T(8,128)(2,1)S(1)} %collective-permute-done.3.refs_4_), channel_id=1, source_target_pairs={{0,1},{1,0},{2,3},{3,2},{4,5},{5,4},{6,7},{7,6},{8,9},{9,8},{10,11... | collective-permute-start | bytes 2359304 | tf_op jit(solution)/shard_map/ppermute | solution.py:25
  76.0 0.2 collective-permute-done.1.refs_2_
  76.1 2.2 %collective-permute-start.2 = (bf16[16,192,128]{2,1,0:T(8,128)(2,1)S(1)}, bf16[16,192,128]{2,1,0:T(8,128)(2,1)}, u32[]{:S(2)}, u32[]{:S(2)}) collective-permute-start(bf16[16,192,128]{2,1,0:T(8,128)(2,1)S(1)} %collective-permute-done.1.refs_2_), channel_id=1, source_target_pairs={{0,1},{1,0},{2,3},{3,2},{4,5},{5,4},{6,7},{7,6},{8,9},{9,8},{10,11... | collective-permute-start | bytes 2359304 | tf_op jit(solution)/shard_map/ppermute | solution.py:25
  78.4 0.1 add_convert_fusion.usable_ref
  78.5 0.0 collective-permute-done.refs_1_
  78.5 0.9 copy-done.3
  79.4 14.6 %all-to-all-done.1.q_ref = bf16[16,96,128]{2,1,0:T(8,128)(2,1)S(1)} async-done(((bf16[16,96,128]{2,1,0:T(8,128)(2,1)}), bf16[16,96,128]{2,1,0:T(8,128)(2,1)S(1)}, u32[]{:S(2)}, u32[]{:S(2)}) %all-to-all-start.1) | async-done | bytes 393248 | tf_op jit(solution)/shard_map/all_to_all | solution.py:237
  94.0 0.0 collective-permute-done.2.refs_3_
  94.0 1.1 copy-done.4
  95.1 19.1 %attend.1 = bf16[16,96,128]{2,1,0:T(8,128)(2,1)} custom-call(s32[2]{0:T(128)S(1)} %add_convert_fusion.usable_ref, bf16[16,96,128]{2,1,0:T(8,128)(2,1)S(1)} %all-to-all-done.1.q_ref, bf16[16,192,128]{2,1,0:T(8,128)(2,1)S(1)} %all-to-all-done.refs_0_, bf16[16,192,128]{2,1,0:T(8,128)(2,1)S(1)} %copy-done.4, ...), custom_call_target="tpu_custom_call" | custom-call | flops 7247757312 | bytes 5505024 | tf_op jit(solution)/shard_map/attend/pallas_call | solution.py:149
  114.2 6.6 %all-to-all-start.2 = ((bf16[16,96,128]{2,1,0:T(8,128)(2,1)}), bf16[16,96,128]{2,1,0:T(8,128)(2,1)S(1)}, u32[]{:S(2)}, u32[]{:S(2)}) async-start(bf16[16,96,128]{2,1,0:T(8,128)(2,1)} %attend.1), calls=%async_computation.2 | async-start | bytes 786432 | tf_op jit(solution)/shard_map/all_to_all | solution.py:241
  121.5 22.6 %all-to-all-done.2.returned_ref = bf16[16,96,128]{2,1,0:T(8,128)(2,1)S(1)} async-done(((bf16[16,96,128]{2,1,0:T(8,128)(2,1)}), bf16[16,96,128]{2,1,0:T(8,128)(2,1)S(1)}, u32[]{:S(2)}, u32[]{:S(2)}) %all-to-all-start.2) | async-done | bytes 393248 | tf_op jit(solution)/shard_map/all_to_all | solution.py:241
  144.1 0.2 update.1
  144.3 0.7 collective-permute-start.6
  145.0 0.7 collective-permute-start.7
  145.7 0.7 collective-permute-start.8
  146.4 8.5 %collective-permute-start.5 = (bf16[1,96,2048]{2,1,0:T(8,128)(2,1)S(1)}, bf16[1,96,2048]{2,1,0:T(8,128)(2,1)S(1)}, u32[]{:S(2)}, u32[]{:S(2)}) collective-permute-start(bf16[1,96,2048]{2,1,0:T(8,128)(2,1)S(1)} %get-tuple-element.11), channel_id=1, source_target_pairs={{0,480},{32,0},{64,32},{96,64},{128,96},{160,128},{192,160},{224,1... | collective-permute-start | bytes 1179656 | tf_op jit(solution)/shard_map/ppermute | solution.py:244
  154.9 0.0 collective-permute-done.7
  155.0 0.7 collective-permute-start.11
  155.6 0.7 collective-permute-start.10
  156.3 1.3 collective-permute-start.9
  157.6 4.4 %collective-permute-done.9.refs_0_ = bf16[96,128]{1,0:T(8,128)(2,1)S(1)} collective-permute-done((bf16[96,128]{1,0:T(8,128)(2,1)S(1)}, bf16[96,128]{1,0:T(8,128)(2,1)S(1)}, u32[]{:S(2)}, u32[]{:S(2)}) %collective-permute-start.9) | collective-permute-done | bytes 24608 | tf_op jit(solution)/shard_map/ppermute | solution.py:222
  162.0 0.8 finish.1
  (16 shorter events, 0.1 us)
Async XLA Ops:
  3.5 54.5 %all-to-all-start = ((bf16[16,192,128]{2,1,0:T(8,128)(2,1)}), bf16[16,192,128]{2,1,0:T(8,128)(2,1)S(1)}, u32[]{:S(2)}, u32[]{:S(2)}) async-start(bf16[16,192,128]{2,1,0:T(8,128)(2,1)} %pack.2), calls=%async_computation | async-start | bytes 1572864 | tf_op jit(solution)/shard_map/all_to_all | solution.py:231
  58.0 16.1 %collective-permute-start.3 = (bf16[16,192,128]{2,1,0:T(8,128)(2,1)S(1)}, bf16[16,192,128]{2,1,0:T(8,128)(2,1)S(1)}, u32[]{:S(2)}, u32[]{:S(2)}) collective-permute-start(bf16[16,192,128]{2,1,0:T(8,128)(2,1)S(1)} %all-to-all-done.refs_0_), channel_id=1, source_target_pairs={{32,0},{64,32},{96,64},{128,96},{160,128},{192,160},{224,192},{256... | collective-permute-start | bytes 2359304 | tf_op jit(solution)/shard_map/ppermute | solution.py:21
  60.3 15.8 %collective-permute-start.1 = (bf16[16,192,128]{2,1,0:T(8,128)(2,1)S(1)}, bf16[16,192,128]{2,1,0:T(8,128)(2,1)S(1)}, u32[]{:S(2)}, u32[]{:S(2)}) collective-permute-start(bf16[16,192,128]{2,1,0:T(8,128)(2,1)S(1)} %all-to-all-done.refs_0_), channel_id=1, source_target_pairs={{0,32},{32,64},{64,96},{96,128},{128,160},{160,192},{192,224},{224... | collective-permute-start | bytes 2359304 | tf_op jit(solution)/shard_map/ppermute | solution.py:21
  63.8 30.1 %all-to-all-start.1 = ((bf16[16,96,128]{2,1,0:T(8,128)(2,1)}), bf16[16,96,128]{2,1,0:T(8,128)(2,1)S(1)}, u32[]{:S(2)}, u32[]{:S(2)}) async-start(bf16[16,96,128]{2,1,0:T(8,128)(2,1)} %pack.3), calls=%async_computation.1 | async-start | bytes 786432 | tf_op jit(solution)/shard_map/all_to_all | solution.py:237
  71.1 7.3 %collective-permute-start = (bf16[16,192,128]{2,1,0:T(8,128)(2,1)S(1)}, bf16[16,192,128]{2,1,0:T(8,128)(2,1)S(1)}, u32[]{:S(2)}, u32[]{:S(2)}) collective-permute-start(bf16[16,192,128]{2,1,0:T(8,128)(2,1)S(1)} %all-to-all-done.refs_0_), channel_id=1, source_target_pairs={{0,1},{1,0},{2,3},{3,2},{4,5},{5,4},{6,7},{7,6},{8,9},{9,8},{10,11... | collective-permute-start | bytes 2359304 | tf_op jit(solution)/shard_map/ppermute | solution.py:25
  74.0 19.9 %collective-permute-start.4 = (bf16[16,192,128]{2,1,0:T(8,128)(2,1)S(1)}, bf16[16,192,128]{2,1,0:T(8,128)(2,1)}, u32[]{:S(2)}, u32[]{:S(2)}) collective-permute-start(bf16[16,192,128]{2,1,0:T(8,128)(2,1)S(1)} %collective-permute-done.3.refs_4_), channel_id=1, source_target_pairs={{0,1},{1,0},{2,3},{3,2},{4,5},{5,4},{6,7},{7,6},{8,9},{9,8},{10,11... | collective-permute-start | bytes 2359304 | tf_op jit(solution)/shard_map/ppermute | solution.py:25
  76.1 17.8 %collective-permute-start.2 = (bf16[16,192,128]{2,1,0:T(8,128)(2,1)S(1)}, bf16[16,192,128]{2,1,0:T(8,128)(2,1)}, u32[]{:S(2)}, u32[]{:S(2)}) collective-permute-start(bf16[16,192,128]{2,1,0:T(8,128)(2,1)S(1)} %collective-permute-done.1.refs_2_), channel_id=1, source_target_pairs={{0,1},{1,0},{2,3},{3,2},{4,5},{5,4},{6,7},{7,6},{8,9},{9,8},{10,11... | collective-permute-start | bytes 2359304 | tf_op jit(solution)/shard_map/ppermute | solution.py:25
  78.5 0.9 copy-start.3
  94.0 1.1 copy-start.4
  95.1 49.0 %copy-start.1 = (bf16[1,96,2048]{2,1,0:T(8,128)(2,1)S(1)}, bf16[1,96,2048]{2,1,0:T(8,128)(2,1)}, u32[]{:S(2)}) copy-start(bf16[1,96,2048]{2,1,0:T(8,128)(2,1)} %residual_ref.1) | copy-start | bytes 1179652
  95.1 49.0 %copy-start.2 = (bf16[96,2048]{1,0:T(8,128)(2,1)S(1)}, bf16[96,2048]{1,0:T(8,128)(2,1)}, u32[]{:S(2)}) copy-start(bf16[96,2048]{1,0:T(8,128)(2,1)} %incoming_ref.1) | copy-start | bytes 1179652
  114.2 29.9 %copy-start = (f32[50,2048]{1,0:T(8,128)S(1)}, f32[50,2048]{1,0:T(8,128)}, u32[]{:S(2)}) copy-start(f32[50,2048]{1,0:T(8,128)} %gate_ref.1) | copy-start | bytes 1228804
  114.2 29.9 %all-to-all-start.2 = ((bf16[16,96,128]{2,1,0:T(8,128)(2,1)}), bf16[16,96,128]{2,1,0:T(8,128)(2,1)S(1)}, u32[]{:S(2)}, u32[]{:S(2)}) async-start(bf16[16,96,128]{2,1,0:T(8,128)(2,1)} %attend.1), calls=%async_computation.2 | async-start | bytes 786432 | tf_op jit(solution)/shard_map/all_to_all | solution.py:241
  144.3 10.6 %collective-permute-start.6 = (bf16[4,96,128]{2,1,0:T(8,128)(2,1)S(1)}, bf16[4,96,128]{2,1,0:T(8,128)(2,1)S(1)}, u32[]{:S(2)}, u32[]{:S(2)}) collective-permute-start(bf16[4,96,128]{2,1,0:T(8,128)(2,1)S(1)} %get-tuple-element.13), channel_id=1, source_target_pairs={{0,128},{1,129},{2,130},{3,131},{4,132},{5,133},{6,134},{7,135},{8... | collective-permute-start | bytes 294920 | tf_op jit(solution)/shard_map/ppermute | solution.py:219
  145.0 9.9 %collective-permute-start.7 = (bf16[4,96,128]{2,1,0:T(8,128)(2,1)S(1)}, bf16[4,96,128]{2,1,0:T(8,128)(2,1)S(1)}, u32[]{:S(2)}, u32[]{:S(2)}) collective-permute-start(bf16[4,96,128]{2,1,0:T(8,128)(2,1)S(1)} %get-tuple-element.14), channel_id=1, source_target_pairs={{0,256},{1,257},{2,258},{3,259},{4,260},{5,261},{6,262},{7,263},{8... | collective-permute-start | bytes 294920 | tf_op jit(solution)/shard_map/ppermute | solution.py:219
  145.7 9.2 %collective-permute-start.8 = (bf16[4,96,128]{2,1,0:T(8,128)(2,1)S(1)}, bf16[4,96,128]{2,1,0:T(8,128)(2,1)S(1)}, u32[]{:S(2)}, u32[]{:S(2)}) collective-permute-start(bf16[4,96,128]{2,1,0:T(8,128)(2,1)S(1)} %get-tuple-element.15), channel_id=1, source_target_pairs={{0,384},{1,385},{2,386},{3,387},{4,388},{5,389},{6,390},{7,391},{8... | collective-permute-start | bytes 294920 | tf_op jit(solution)/shard_map/ppermute | solution.py:219
  146.4 15.7 %collective-permute-start.5 = (bf16[1,96,2048]{2,1,0:T(8,128)(2,1)S(1)}, bf16[1,96,2048]{2,1,0:T(8,128)(2,1)S(1)}, u32[]{:S(2)}, u32[]{:S(2)}) collective-permute-start(bf16[1,96,2048]{2,1,0:T(8,128)(2,1)S(1)} %get-tuple-element.11), channel_id=1, source_target_pairs={{0,480},{32,0},{64,32},{96,64},{128,96},{160,128},{192,160},{224,1... | collective-permute-start | bytes 1179656 | tf_op jit(solution)/shard_map/ppermute | solution.py:244
  155.0 2.7 %collective-permute-start.11 = (bf16[96,128]{1,0:T(8,128)(2,1)S(1)}, bf16[96,128]{1,0:T(8,128)(2,1)S(1)}, u32[]{:S(2)}, u32[]{:S(2)}) collective-permute-start(bf16[96,128]{1,0:T(8,128)(2,1)S(1)} %get-tuple-element.16), channel_id=1, source_target_pairs={{0,96},{128,224},{256,352},{384,480},{1,97},{129,225},{257,353},{3... | collective-permute-start | bytes 73736 | tf_op jit(solution)/shard_map/ppermute | solution.py:222
  155.6 2.0 %collective-permute-start.10 = (bf16[96,128]{1,0:T(8,128)(2,1)S(1)}, bf16[96,128]{1,0:T(8,128)(2,1)S(1)}, u32[]{:S(2)}, u32[]{:S(2)}) collective-permute-start(bf16[96,128]{1,0:T(8,128)(2,1)S(1)} %get-tuple-element.17), channel_id=1, source_target_pairs={{0,64},{128,192},{256,320},{384,448},{1,65},{129,193},{257,321},{3... | collective-permute-start | bytes 73736 | tf_op jit(solution)/shard_map/ppermute | solution.py:222
  156.3 5.7 %collective-permute-start.9 = (bf16[96,128]{1,0:T(8,128)(2,1)S(1)}, bf16[96,128]{1,0:T(8,128)(2,1)S(1)}, u32[]{:S(2)}, u32[]{:S(2)}) collective-permute-start(bf16[96,128]{1,0:T(8,128)(2,1)S(1)} %get-tuple-element.18), channel_id=1, source_target_pairs={{0,32},{128,160},{256,288},{384,416},{1,33},{129,161},{257,289},{3... | collective-permute-start | bytes 73736 | tf_op jit(solution)/shard_map/ppermute | solution.py:222

commit v3 on v2

--- a/solution.py
+++ b/solution.py
@@ -151,7 +151,7 @@
         out_shape=jax.ShapeDtypeStruct(q.shape, jnp.bfloat16),
         in_specs=[SMEM] + [VMEM] * (1 + len(pairs)),
         out_specs=VMEM,
-        compiler_params=pltpu.CompilerParams(vmem_limit_bytes=26 * 2**20),
+        compiler_params=pltpu.CompilerParams(vmem_limit_bytes=60 * 2**20),
         cost_estimate=pl.CostEstimate(
             flops=24 * rows * rows * HD,
             bytes_accessed=28 * rows * HD,
@@ -237,7 +237,7 @@
     q = lax.all_to_all(packed, "head", split_axis=0, concat_axis=0, tiled=True)
     pairs = (own, swapped(own), prior, swapped(prior), later, swapped(later))
     usable = jnp.stack([frame_index > 0, frame_index < frames - 1]).astype(jnp.int32)
-    attention = attend(usable, q, pairs, query_rows=384)
+    attention = attend(usable, q, pairs, query_rows=768)
     returned = lax.all_to_all(attention, "head", split_axis=0, concat_axis=0, tiled=True)
     first = (frame_index == 0).astype(jnp.int32)[None]
     moving, parts = update(timesteps, first, returned, residual, incoming, gate_table)

time: 164 us -> 164 us (level)
  no operation moved by 1% of the time
where the time goes in v3:
time: 164 us; the launch traced here: 163 us
  waiting for transfers between devices  80.3 us (49%)
  starting transfers between devices  54.2 us (33%)
  Pallas kernels  24.9 us (15%)
  between operations  2.18 us (1%)
    all_to_all x1, waiting for transfers between devices, per_device(): lax.all_to_all(pack(positions, keys, values), 'head', split_axis=0, conca...  37.3 us
    all_to_all x1, waiting for transfers between devices, per_device(): lax.all_to_all(attention, 'head', split_axis=0, concat_axis=0, tiled=True)  22.6 us
    pallas_call x1, Pallas kernels, attend(): pl.pallas_call(functools.partial(attend_kernel, **sizes), out_shape=jax.S...  19.8 us
    all_to_all x1, starting transfers between devices, per_device(): lax.all_to_all(pack(positions, keys, values), 'head', split_axis=0, conca...  15.2 us
    all_to_all x1, waiting for transfers between devices, per_device(): q = lax.all_to_all(packed, 'head', split_axis=0, concat_axis=0, tiled=True)  14.9 us
    ppermute x1, starting transfers between devices, per_device(): lax.ppermute(moving, 'frame', [(i, (i - 1) % frames) for i in range(frame...  8.52 us
    all_to_all x1, starting transfers between devices, per_device(): q = lax.all_to_all(packed, 'head', split_axis=0, concat_axis=0, tiled=True)  7.32 us
    all_to_all x1, starting transfers between devices, per_device(): lax.all_to_all(attention, 'head', split_axis=0, concat_axis=0, tiled=True)  6.64 us
  transfers between devices with their start and end apart: 15, of which 6 were waited for; matrix products, arithmetic and copies ran while one was open for 0% of the time, Pallas kernels for 1%

profile of v3, /device:TPU:8, one launch (start us, length us, event | category | flops | bytes accessed | tf_op | source)
XLA Modules:
  0.0 163.1 jit_solution(6675671412161512011)
XLA Ops:
  1.3 2.2 %pack.2 = bf16[16,192,128]{2,1,0:T(8,128)(2,1)} custom-call(s32[1]{0:T(128)S(6)} %copy.11.position_ref, bf16[1,96,2048]{2,1,0:T(8,128)(2,1)} %turned_ref.2, bf16[1,96,2048]{2,1,0:T(8,128)(2,1)} %refs_0_.1), custom_call_target="tpu_custom_call" | custom-call | tf_op jit(solution)/shard_map/pack/pallas_call | solution.py:65
  3.5 15.2 %all-to-all-start = ((bf16[16,192,128]{2,1,0:T(8,128)(2,1)}), bf16[16,192,128]{2,1,0:T(8,128)(2,1)S(1)}, u32[]{:S(2)}, u32[]{:S(2)}) async-start(bf16[16,192,128]{2,1,0:T(8,128)(2,1)} %pack.2), calls=%async_computation | async-start | bytes 1572864 | tf_op jit(solution)/shard_map/all_to_all | solution.py:231
  18.7 2.0 %pack.3 = bf16[16,96,128]{2,1,0:T(8,128)(2,1)} custom-call(s32[1]{0:T(128)S(6)} %copy.11.position_ref, bf16[1,96,2048]{2,1,0:T(8,128)(2,1)} %turned_ref.3), custom_call_target="tpu_custom_call" | custom-call | tf_op jit(solution)/shard_map/pack/pallas_call | solution.py:65
  20.7 37.3 %all-to-all-done.refs_0_ = bf16[16,192,128]{2,1,0:T(8,128)(2,1)S(1)} async-done(((bf16[16,192,128]{2,1,0:T(8,128)(2,1)}), bf16[16,192,128]{2,1,0:T(8,128)(2,1)S(1)}, u32[]{:S(2)}, u32[]{:S(2)}) %all-to-all-start) | async-done | bytes 786464 | tf_op jit(solution)/shard_map/all_to_all | solution.py:231
  58.0 2.3 %collective-permute-start.3 = (bf16[16,192,128]{2,1,0:T(8,128)(2,1)S(1)}, bf16[16,192,128]{2,1,0:T(8,128)(2,1)S(1)}, u32[]{:S(2)}, u32[]{:S(2)}) collective-permute-start(bf16[16,192,128]{2,1,0:T(8,128)(2,1)S(1)} %all-to-all-done.refs_0_), channel_id=1, source_target_pairs={{32,0},{64,32},{96,64},{128,96},{160,128},{192,160},{224,192},{256... | collective-permute-start | bytes 2359304 | tf_op jit(solution)/shard_map/ppermute | solution.py:21
  60.3 3.5 %collective-permute-start.1 = (bf16[16,192,128]{2,1,0:T(8,128)(2,1)S(1)}, bf16[16,192,128]{2,1,0:T(8,128)(2,1)S(1)}, u32[]{:S(2)}, u32[]{:S(2)}) collective-permute-start(bf16[16,192,128]{2,1,0:T(8,128)(2,1)S(1)} %all-to-all-done.refs_0_), channel_id=1, source_target_pairs={{0,32},{32,64},{64,96},{96,128},{128,160},{160,192},{192,224},{224... | collective-permute-start | bytes 2359304 | tf_op jit(solution)/shard_map/ppermute | solution.py:21
  63.8 7.3 %all-to-all-start.1 = ((bf16[16,96,128]{2,1,0:T(8,128)(2,1)}), bf16[16,96,128]{2,1,0:T(8,128)(2,1)S(1)}, u32[]{:S(2)}, u32[]{:S(2)}) async-start(bf16[16,96,128]{2,1,0:T(8,128)(2,1)} %pack.3), calls=%async_computation.1 | async-start | bytes 786432 | tf_op jit(solution)/shard_map/all_to_all | solution.py:237
  71.2 1.9 %collective-permute-start = (bf16[16,192,128]{2,1,0:T(8,128)(2,1)S(1)}, bf16[16,192,128]{2,1,0:T(8,128)(2,1)S(1)}, u32[]{:S(2)}, u32[]{:S(2)}) collective-permute-start(bf16[16,192,128]{2,1,0:T(8,128)(2,1)S(1)} %all-to-all-done.refs_0_), channel_id=1, source_target_pairs={{0,1},{1,0},{2,3},{3,2},{4,5},{5,4},{6,7},{7,6},{8,9},{9,8},{10,11... | collective-permute-start | bytes 2359304 | tf_op jit(solution)/shard_map/ppermute | solution.py:25
  73.1 1.0 collective-permute-done.3.refs_4_
  74.0 1.9 %collective-permute-start.4 = (bf16[16,192,128]{2,1,0:T(8,128)(2,1)S(1)}, bf16[16,192,128]{2,1,0:T(8,128)(2,1)}, u32[]{:S(2)}, u32[]{:S(2)}) collective-permute-start(bf16[16,192,128]{2,1,0:T(8,128)(2,1)S(1)} %collective-permute-done.3.refs_4_), channel_id=1, source_target_pairs={{0,1},{1,0},{2,3},{3,2},{4,5},{5,4},{6,7},{7,6},{8,9},{9,8},{10,11... | collective-permute-start | bytes 2359304 | tf_op jit(solution)/shard_map/ppermute | solution.py:25
  76.0 0.2 collective-permute-done.1.refs_2_
  76.1 2.3 %collective-permute-start.2 = (bf16[16,192,128]{2,1,0:T(8,128)(2,1)S(1)}, bf16[16,192,128]{2,1,0:T(8,128)(2,1)}, u32[]{:S(2)}, u32[]{:S(2)}) collective-permute-start(bf16[16,192,128]{2,1,0:T(8,128)(2,1)S(1)} %collective-permute-done.1.refs_2_), channel_id=1, source_target_pairs={{0,1},{1,0},{2,3},{3,2},{4,5},{5,4},{6,7},{7,6},{8,9},{9,8},{10,11... | collective-permute-start | bytes 2359304 | tf_op jit(solution)/shard_map/ppermute | solution.py:25
  78.4 0.7 add_convert_fusion.usable_ref
  79.1 0.0 collective-permute-done.refs_1_
  79.1 14.9 %all-to-all-done.1.q_ref = bf16[16,96,128]{2,1,0:T(8,128)(2,1)S(1)} async-done(((bf16[16,96,128]{2,1,0:T(8,128)(2,1)}), bf16[16,96,128]{2,1,0:T(8,128)(2,1)S(1)}, u32[]{:S(2)}, u32[]{:S(2)}) %all-to-all-start.1) | async-done | bytes 393248 | tf_op jit(solution)/shard_map/all_to_all | solution.py:237
  94.0 0.7 copy-done.4
  94.7 19.8 %attend.1 = bf16[16,96,128]{2,1,0:T(8,128)(2,1)} custom-call(s32[2]{0:T(128)} %add_convert_fusion.usable_ref, bf16[16,96,128]{2,1,0:T(8,128)(2,1)} %copy-done.4, bf16[16,192,128]{2,1,0:T(8,128)(2,1)} %copy-done.3, bf16[16,192,128]{2,1,0:T(8,128)(2,1)} %copy-done.7, bf16[16,192,128]{2,1,0:T(8,128)(2,1)} %copy-done.6, ...), custom_call_target="tpu_custom_call" | custom-call | flops 7247757312 | bytes 5505024 | tf_op jit(solution)/shard_map/attend/pallas_call | solution.py:149
  114.5 6.6 %all-to-all-start.2 = ((bf16[16,96,128]{2,1,0:T(8,128)(2,1)}), bf16[16,96,128]{2,1,0:T(8,128)(2,1)S(1)}, u32[]{:S(2)}, u32[]{:S(2)}) async-start(bf16[16,96,128]{2,1,0:T(8,128)(2,1)} %attend.1), calls=%async_computation.2 | async-start | bytes 786432 | tf_op jit(solution)/shard_map/all_to_all | solution.py:241
  121.8 22.6 %all-to-all-done.2.returned_ref = bf16[16,96,128]{2,1,0:T(8,128)(2,1)S(1)} async-done(((bf16[16,96,128]{2,1,0:T(8,128)(2,1)}), bf16[16,96,128]{2,1,0:T(8,128)(2,1)S(1)}, u32[]{:S(2)}, u32[]{:S(2)}) %all-to-all-start.2) | async-done | bytes 393248 | tf_op jit(solution)/shard_map/all_to_all | solution.py:241
  144.4 0.2 update.1
  144.6 0.7 collective-permute-start.6
  145.3 0.7 collective-permute-start.7
  145.9 0.7 collective-permute-start.8
  146.6 8.5 %collective-permute-start.5 = (bf16[1,96,2048]{2,1,0:T(8,128)(2,1)S(1)}, bf16[1,96,2048]{2,1,0:T(8,128)(2,1)S(1)}, u32[]{:S(2)}, u32[]{:S(2)}) collective-permute-start(bf16[1,96,2048]{2,1,0:T(8,128)(2,1)S(1)} %get-tuple-element.11), channel_id=1, source_target_pairs={{0,480},{32,0},{64,32},{96,64},{128,96},{160,128},{192,160},{224,1... | collective-permute-start | bytes 1179656 | tf_op jit(solution)/shard_map/ppermute | solution.py:244
  155.1 0.0 collective-permute-done.6
  155.1 0.0 collective-permute-done.7
  155.2 0.7 collective-permute-start.11
  155.9 0.7 collective-permute-start.10
  156.6 1.3 collective-permute-start.9
  157.9 0.0 collective-permute-done.10.refs_1_
  157.9 4.4 %collective-permute-done.9.refs_0_ = bf16[96,128]{1,0:T(8,128)(2,1)S(1)} collective-permute-done((bf16[96,128]{1,0:T(8,128)(2,1)S(1)}, bf16[96,128]{1,0:T(8,128)(2,1)S(1)}, u32[]{:S(2)}, u32[]{:S(2)}) %collective-permute-start.9) | collective-permute-done | bytes 24608 | tf_op jit(solution)/shard_map/ppermute | solution.py:222
  162.3 0.8 finish.1
  (22 shorter events, 0.1 us)
Async XLA Ops:
  3.5 54.5 %all-to-all-start = ((bf16[16,192,128]{2,1,0:T(8,128)(2,1)}), bf16[16,192,128]{2,1,0:T(8,128)(2,1)S(1)}, u32[]{:S(2)}, u32[]{:S(2)}) async-start(bf16[16,192,128]{2,1,0:T(8,128)(2,1)} %pack.2), calls=%async_computation | async-start | bytes 1572864 | tf_op jit(solution)/shard_map/all_to_all | solution.py:231
  58.0 36.0 %copy-start.3 = (bf16[16,192,128]{2,1,0:T(8,128)(2,1)}, bf16[16,192,128]{2,1,0:T(8,128)(2,1)S(1)}, u32[]{:S(2)}) copy-start(bf16[16,192,128]{2,1,0:T(8,128)(2,1)S(1)} %all-to-all-done.refs_0_) | copy-start | bytes 2359300
  58.0 16.1 %collective-permute-start.3 = (bf16[16,192,128]{2,1,0:T(8,128)(2,1)S(1)}, bf16[16,192,128]{2,1,0:T(8,128)(2,1)S(1)}, u32[]{:S(2)}, u32[]{:S(2)}) collective-permute-start(bf16[16,192,128]{2,1,0:T(8,128)(2,1)S(1)} %all-to-all-done.refs_0_), channel_id=1, source_target_pairs={{32,0},{64,32},{96,64},{128,96},{160,128},{192,160},{224,192},{256... | collective-permute-start | bytes 2359304 | tf_op jit(solution)/shard_map/ppermute | solution.py:21
  60.3 15.8 %collective-permute-start.1 = (bf16[16,192,128]{2,1,0:T(8,128)(2,1)S(1)}, bf16[16,192,128]{2,1,0:T(8,128)(2,1)S(1)}, u32[]{:S(2)}, u32[]{:S(2)}) collective-permute-start(bf16[16,192,128]{2,1,0:T(8,128)(2,1)S(1)} %all-to-all-done.refs_0_), channel_id=1, source_target_pairs={{0,32},{32,64},{64,96},{96,128},{128,160},{160,192},{192,224},{224... | collective-permute-start | bytes 2359304 | tf_op jit(solution)/shard_map/ppermute | solution.py:21
  63.8 30.1 %all-to-all-start.1 = ((bf16[16,96,128]{2,1,0:T(8,128)(2,1)}), bf16[16,96,128]{2,1,0:T(8,128)(2,1)S(1)}, u32[]{:S(2)}, u32[]{:S(2)}) async-start(bf16[16,96,128]{2,1,0:T(8,128)(2,1)} %pack.3), calls=%async_computation.1 | async-start | bytes 786432 | tf_op jit(solution)/shard_map/all_to_all | solution.py:237
  71.2 7.9 %collective-permute-start = (bf16[16,192,128]{2,1,0:T(8,128)(2,1)S(1)}, bf16[16,192,128]{2,1,0:T(8,128)(2,1)S(1)}, u32[]{:S(2)}, u32[]{:S(2)}) collective-permute-start(bf16[16,192,128]{2,1,0:T(8,128)(2,1)S(1)} %all-to-all-done.refs_0_), channel_id=1, source_target_pairs={{0,1},{1,0},{2,3},{3,2},{4,5},{5,4},{6,7},{7,6},{8,9},{9,8},{10,11... | collective-permute-start | bytes 2359304 | tf_op jit(solution)/shard_map/ppermute | solution.py:25
  74.0 20.0 %copy-start.5 = (bf16[16,192,128]{2,1,0:T(8,128)(2,1)}, bf16[16,192,128]{2,1,0:T(8,128)(2,1)S(1)}, u32[]{:S(2)}) copy-start(bf16[16,192,128]{2,1,0:T(8,128)(2,1)S(1)} %collective-permute-done.3.refs_4_) | copy-start | bytes 2359300
  74.0 19.9 %collective-permute-start.4 = (bf16[16,192,128]{2,1,0:T(8,128)(2,1)S(1)}, bf16[16,192,128]{2,1,0:T(8,128)(2,1)}, u32[]{:S(2)}, u32[]{:S(2)}) collective-permute-start(bf16[16,192,128]{2,1,0:T(8,128)(2,1)S(1)} %collective-permute-done.3.refs_4_), channel_id=1, source_target_pairs={{0,1},{1,0},{2,3},{3,2},{4,5},{5,4},{6,7},{7,6},{8,9},{9,8},{10,11... | collective-permute-start | bytes 2359304 | tf_op jit(solution)/shard_map/ppermute | solution.py:25
  76.1 17.9 %copy-start.6 = (bf16[16,192,128]{2,1,0:T(8,128)(2,1)}, bf16[16,192,128]{2,1,0:T(8,128)(2,1)S(1)}, u32[]{:S(2)}) copy-start(bf16[16,192,128]{2,1,0:T(8,128)(2,1)S(1)} %collective-permute-done.1.refs_2_) | copy-start | bytes 2359300
  76.1 17.9 %collective-permute-start.2 = (bf16[16,192,128]{2,1,0:T(8,128)(2,1)S(1)}, bf16[16,192,128]{2,1,0:T(8,128)(2,1)}, u32[]{:S(2)}, u32[]{:S(2)}) collective-permute-start(bf16[16,192,128]{2,1,0:T(8,128)(2,1)S(1)} %collective-permute-done.1.refs_2_), channel_id=1, source_target_pairs={{0,1},{1,0},{2,3},{3,2},{4,5},{5,4},{6,7},{7,6},{8,9},{9,8},{10,11... | collective-permute-start | bytes 2359304 | tf_op jit(solution)/shard_map/ppermute | solution.py:25
  79.1 14.9 %copy-start.7 = (bf16[16,192,128]{2,1,0:T(8,128)(2,1)}, bf16[16,192,128]{2,1,0:T(8,128)(2,1)S(1)}, u32[]{:S(2)}) copy-start(bf16[16,192,128]{2,1,0:T(8,128)(2,1)S(1)} %collective-permute-done.refs_1_) | copy-start | bytes 2359300
  94.0 0.7 copy-start.4
  94.7 49.7 %copy-start.1 = (bf16[1,96,2048]{2,1,0:T(8,128)(2,1)S(1)}, bf16[1,96,2048]{2,1,0:T(8,128)(2,1)}, u32[]{:S(2)}) copy-start(bf16[1,96,2048]{2,1,0:T(8,128)(2,1)} %residual_ref.1) | copy-start | bytes 1179652
  94.7 49.7 %copy-start.2 = (bf16[96,2048]{1,0:T(8,128)(2,1)S(1)}, bf16[96,2048]{1,0:T(8,128)(2,1)}, u32[]{:S(2)}) copy-start(bf16[96,2048]{1,0:T(8,128)(2,1)} %incoming_ref.1) | copy-start | bytes 1179652
  114.5 29.9 %copy-start = (f32[50,2048]{1,0:T(8,128)S(1)}, f32[50,2048]{1,0:T(8,128)}, u32[]{:S(2)}) copy-start(f32[50,2048]{1,0:T(8,128)} %gate_ref.1) | copy-start | bytes 1228804
  114.5 29.9 %all-to-all-start.2 = ((bf16[16,96,128]{2,1,0:T(8,128)(2,1)}), bf16[16,96,128]{2,1,0:T(8,128)(2,1)S(1)}, u32[]{:S(2)}, u32[]{:S(2)}) async-start(bf16[16,96,128]{2,1,0:T(8,128)(2,1)} %attend.1), calls=%async_computation.2 | async-start | bytes 786432 | tf_op jit(solution)/shard_map/all_to_all | solution.py:241
  144.6 10.6 %collective-permute-start.6 = (bf16[4,96,128]{2,1,0:T(8,128)(2,1)S(1)}, bf16[4,96,128]{2,1,0:T(8,128)(2,1)S(1)}, u32[]{:S(2)}, u32[]{:S(2)}) collective-permute-start(bf16[4,96,128]{2,1,0:T(8,128)(2,1)S(1)} %get-tuple-element.13), channel_id=1, source_target_pairs={{0,128},{1,129},{2,130},{3,131},{4,132},{5,133},{6,134},{7,135},{8... | collective-permute-start | bytes 294920 | tf_op jit(solution)/shard_map/ppermute | solution.py:219
  145.3 9.9 %collective-permute-start.7 = (bf16[4,96,128]{2,1,0:T(8,128)(2,1)S(1)}, bf16[4,96,128]{2,1,0:T(8,128)(2,1)S(1)}, u32[]{:S(2)}, u32[]{:S(2)}) collective-permute-start(bf16[4,96,128]{2,1,0:T(8,128)(2,1)S(1)} %get-tuple-element.14), channel_id=1, source_target_pairs={{0,256},{1,257},{2,258},{3,259},{4,260},{5,261},{6,262},{7,263},{8... | collective-permute-start | bytes 294920 | tf_op jit(solution)/shard_map/ppermute | solution.py:219
  145.9 9.2 %collective-permute-start.8 = (bf16[4,96,128]{2,1,0:T(8,128)(2,1)S(1)}, bf16[4,96,128]{2,1,0:T(8,128)(2,1)S(1)}, u32[]{:S(2)}, u32[]{:S(2)}) collective-permute-start(bf16[4,96,128]{2,1,0:T(8,128)(2,1)S(1)} %get-tuple-element.15), channel_id=1, source_target_pairs={{0,384},{1,385},{2,386},{3,387},{4,388},{5,389},{6,390},{7,391},{8... | collective-permute-start | bytes 294920 | tf_op jit(solution)/shard_map/ppermute | solution.py:219
  146.6 15.7 %collective-permute-start.5 = (bf16[1,96,2048]{2,1,0:T(8,128)(2,1)S(1)}, bf16[1,96,2048]{2,1,0:T(8,128)(2,1)S(1)}, u32[]{:S(2)}, u32[]{:S(2)}) collective-permute-start(bf16[1,96,2048]{2,1,0:T(8,128)(2,1)S(1)} %get-tuple-element.11), channel_id=1, source_target_pairs={{0,480},{32,0},{64,32},{96,64},{128,96},{160,128},{192,160},{224,1... | collective-permute-start | bytes 1179656 | tf_op jit(solution)/shard_map/ppermute | solution.py:244
  155.2 2.7 %collective-permute-start.11 = (bf16[96,128]{1,0:T(8,128)(2,1)S(1)}, bf16[96,128]{1,0:T(8,128)(2,1)S(1)}, u32[]{:S(2)}, u32[]{:S(2)}) collective-permute-start(bf16[96,128]{1,0:T(8,128)(2,1)S(1)} %get-tuple-element.16), channel_id=1, source_target_pairs={{0,96},{128,224},{256,352},{384,480},{1,97},{129,225},{257,353},{3... | collective-permute-start | bytes 73736 | tf_op jit(solution)/shard_map/ppermute | solution.py:222
  155.9 2.0 %collective-permute-start.10 = (bf16[96,128]{1,0:T(8,128)(2,1)S(1)}, bf16[96,128]{1,0:T(8,128)(2,1)S(1)}, u32[]{:S(2)}, u32[]{:S(2)}) collective-permute-start(bf16[96,128]{1,0:T(8,128)(2,1)S(1)} %get-tuple-element.17), channel_id=1, source_target_pairs={{0,64},{128,192},{256,320},{384,448},{1,65},{129,193},{257,321},{3... | collective-permute-start | bytes 73736 | tf_op jit(solution)/shard_map/ppermute | solution.py:222
  156.6 5.7 %collective-permute-start.9 = (bf16[96,128]{1,0:T(8,128)(2,1)S(1)}, bf16[96,128]{1,0:T(8,128)(2,1)S(1)}, u32[]{:S(2)}, u32[]{:S(2)}) collective-permute-start(bf16[96,128]{1,0:T(8,128)(2,1)S(1)} %get-tuple-element.18), channel_id=1, source_target_pairs={{0,32},{128,160},{256,288},{384,416},{1,33},{129,161},{257,289},{3... | collective-permute-start | bytes 73736 | tf_op jit(solution)/shard_map/ppermute | solution.py:222

commit v4 on v3

--- a/solution.py
+++ b/solution.py
@@ -151,7 +151,7 @@
         out_shape=jax.ShapeDtypeStruct(q.shape, jnp.bfloat16),
         in_specs=[SMEM] + [VMEM] * (1 + len(pairs)),
         out_specs=VMEM,
-        compiler_params=pltpu.CompilerParams(vmem_limit_bytes=60 * 2**20),
+        compiler_params=pltpu.CompilerParams(vmem_limit_bytes=44 * 2**20),
         cost_estimate=pl.CostEstimate(
             flops=24 * rows * rows * HD,
             bytes_accessed=28 * rows * HD,

time: 164 us -> 163 us (level)
  no operation moved by 1% of the time
where the time goes in v4:
time: 163 us; the launch traced here: 162 us
  waiting for transfers between devices  80.1 us (49%)
  starting transfers between devices  54.2 us (33%)
  Pallas kernels  23.9 us (15%)
  between operations  2.15 us (1%)
  local copies, waits for them, and re-layouts  2.04 us (1%)
    all_to_all x1, waiting for transfers between devices, per_device(): lax.all_to_all(pack(positions, keys, values), 'head', split_axis=0, conca...  37.3 us
    all_to_all x1, waiting for transfers between devices, per_device(): lax.all_to_all(attention, 'head', split_axis=0, concat_axis=0, tiled=True)  22.6 us
    pallas_call x1, Pallas kernels, attend(): pl.pallas_call(functools.partial(attend_kernel, **sizes), out_shape=jax.S...  18.7 us
    all_to_all x1, starting transfers between devices, per_device(): lax.all_to_all(pack(positions, keys, values), 'head', split_axis=0, conca...  15.2 us
    all_to_all x1, waiting for transfers between devices, per_device(): q = lax.all_to_all(packed, 'head', split_axis=0, concat_axis=0, tiled=True)  14.6 us
    ppermute x1, starting transfers between devices, per_device(): lax.ppermute(moving, 'frame', [(i, (i - 1) % frames) for i in range(frame...  8.52 us
    all_to_all x1, starting transfers between devices, per_device(): q = lax.all_to_all(packed, 'head', split_axis=0, concat_axis=0, tiled=True)  7.32 us
    all_to_all x1, starting transfers between devices, per_device(): lax.all_to_all(attention, 'head', split_axis=0, concat_axis=0, tiled=True)  6.64 us
  transfers between devices with their start and end apart: 15, of which 6 were waited for; matrix products, arithmetic and copies ran while one was open for 0% of the time, Pallas kernels for 1%

profile of v4, /device:TPU:8, one launch (start us, length us, event | category | flops | bytes accessed | tf_op | source)
XLA Modules:
  0.0 162.4 jit_solution(3724583027113668653)
XLA Ops:
  1.3 2.2 %pack.2 = bf16[16,192,128]{2,1,0:T(8,128)(2,1)} custom-call(s32[1]{0:T(128)S(6)} %copy.11.position_ref, bf16[1,96,2048]{2,1,0:T(8,128)(2,1)} %turned_ref.2, bf16[1,96,2048]{2,1,0:T(8,128)(2,1)} %refs_0_.1), custom_call_target="tpu_custom_call" | custom-call | tf_op jit(solution)/shard_map/pack/pallas_call | solution.py:65
  3.5 15.2 %all-to-all-start = ((bf16[16,192,128]{2,1,0:T(8,128)(2,1)}), bf16[16,192,128]{2,1,0:T(8,128)(2,1)S(1)}, u32[]{:S(2)}, u32[]{:S(2)}) async-start(bf16[16,192,128]{2,1,0:T(8,128)(2,1)} %pack.2), calls=%async_computation | async-start | bytes 1572864 | tf_op jit(solution)/shard_map/all_to_all | solution.py:231
  18.7 2.0 %pack.3 = bf16[16,96,128]{2,1,0:T(8,128)(2,1)} custom-call(s32[1]{0:T(128)S(6)} %copy.11.position_ref, bf16[1,96,2048]{2,1,0:T(8,128)(2,1)} %turned_ref.3), custom_call_target="tpu_custom_call" | custom-call | tf_op jit(solution)/shard_map/pack/pallas_call | solution.py:65
  20.7 37.3 %all-to-all-done.refs_0_ = bf16[16,192,128]{2,1,0:T(8,128)(2,1)S(1)} async-done(((bf16[16,192,128]{2,1,0:T(8,128)(2,1)}), bf16[16,192,128]{2,1,0:T(8,128)(2,1)S(1)}, u32[]{:S(2)}, u32[]{:S(2)}) %all-to-all-start) | async-done | bytes 786464 | tf_op jit(solution)/shard_map/all_to_all | solution.py:231
  58.0 2.3 %collective-permute-start.3 = (bf16[16,192,128]{2,1,0:T(8,128)(2,1)S(1)}, bf16[16,192,128]{2,1,0:T(8,128)(2,1)S(1)}, u32[]{:S(2)}, u32[]{:S(2)}) collective-permute-start(bf16[16,192,128]{2,1,0:T(8,128)(2,1)S(1)} %all-to-all-done.refs_0_), channel_id=1, source_target_pairs={{32,0},{64,32},{96,64},{128,96},{160,128},{192,160},{224,192},{256... | collective-permute-start | bytes 2359304 | tf_op jit(solution)/shard_map/ppermute | solution.py:21
  60.3 3.5 %collective-permute-start.1 = (bf16[16,192,128]{2,1,0:T(8,128)(2,1)S(1)}, bf16[16,192,128]{2,1,0:T(8,128)(2,1)S(1)}, u32[]{:S(2)}, u32[]{:S(2)}) collective-permute-start(bf16[16,192,128]{2,1,0:T(8,128)(2,1)S(1)} %all-to-all-done.refs_0_), channel_id=1, source_target_pairs={{0,32},{32,64},{64,96},{96,128},{128,160},{160,192},{192,224},{224... | collective-permute-start | bytes 2359304 | tf_op jit(solution)/shard_map/ppermute | solution.py:21
  63.8 7.3 %all-to-all-start.1 = ((bf16[16,96,128]{2,1,0:T(8,128)(2,1)}), bf16[16,96,128]{2,1,0:T(8,128)(2,1)S(1)}, u32[]{:S(2)}, u32[]{:S(2)}) async-start(bf16[16,96,128]{2,1,0:T(8,128)(2,1)} %pack.3), calls=%async_computation.1 | async-start | bytes 786432 | tf_op jit(solution)/shard_map/all_to_all | solution.py:237
  71.1 1.9 %collective-permute-start = (bf16[16,192,128]{2,1,0:T(8,128)(2,1)S(1)}, bf16[16,192,128]{2,1,0:T(8,128)(2,1)S(1)}, u32[]{:S(2)}, u32[]{:S(2)}) collective-permute-start(bf16[16,192,128]{2,1,0:T(8,128)(2,1)S(1)} %all-to-all-done.refs_0_), channel_id=1, source_target_pairs={{0,1},{1,0},{2,3},{3,2},{4,5},{5,4},{6,7},{7,6},{8,9},{9,8},{10,11... | collective-permute-start | bytes 2359304 | tf_op jit(solution)/shard_map/ppermute | solution.py:25
  73.1 1.0 collective-permute-done.3.refs_4_
  74.0 1.9 %collective-permute-start.4 = (bf16[16,192,128]{2,1,0:T(8,128)(2,1)S(1)}, bf16[16,192,128]{2,1,0:T(8,128)(2,1)}, u32[]{:S(2)}, u32[]{:S(2)}) collective-permute-start(bf16[16,192,128]{2,1,0:T(8,128)(2,1)S(1)} %collective-permute-done.3.refs_4_), channel_id=1, source_target_pairs={{0,1},{1,0},{2,3},{3,2},{4,5},{5,4},{6,7},{7,6},{8,9},{9,8},{10,11... | collective-permute-start | bytes 2359304 | tf_op jit(solution)/shard_map/ppermute | solution.py:25
  76.0 0.2 collective-permute-done.1.refs_2_
  76.1 2.2 %collective-permute-start.2 = (bf16[16,192,128]{2,1,0:T(8,128)(2,1)S(1)}, bf16[16,192,128]{2,1,0:T(8,128)(2,1)}, u32[]{:S(2)}, u32[]{:S(2)}) collective-permute-start(bf16[16,192,128]{2,1,0:T(8,128)(2,1)S(1)} %collective-permute-done.1.refs_2_), channel_id=1, source_target_pairs={{0,1},{1,0},{2,3},{3,2},{4,5},{5,4},{6,7},{7,6},{8,9},{9,8},{10,11... | collective-permute-start | bytes 2359304 | tf_op jit(solution)/shard_map/ppermute | solution.py:25
  78.4 0.1 add_convert_fusion.usable_ref
  78.5 0.0 collective-permute-done.refs_1_
  78.5 0.9 copy-done.3
  79.4 14.6 %all-to-all-done.1.q_ref = bf16[16,96,128]{2,1,0:T(8,128)(2,1)S(1)} async-done(((bf16[16,96,128]{2,1,0:T(8,128)(2,1)}), bf16[16,96,128]{2,1,0:T(8,128)(2,1)S(1)}, u32[]{:S(2)}, u32[]{:S(2)}) %all-to-all-start.1) | async-done | bytes 393248 | tf_op jit(solution)/shard_map/all_to_all | solution.py:237
  94.0 0.0 collective-permute-done.4.refs_5_
  94.0 0.0 collective-permute-done.2.refs_3_
  94.0 1.1 copy-done.4
  95.1 18.7 %attend.1 = bf16[16,96,128]{2,1,0:T(8,128)(2,1)} custom-call(s32[2]{0:T(128)S(1)} %add_convert_fusion.usable_ref, bf16[16,96,128]{2,1,0:T(8,128)(2,1)S(1)} %all-to-all-done.1.q_ref, bf16[16,192,128]{2,1,0:T(8,128)(2,1)S(1)} %all-to-all-done.refs_0_, bf16[16,192,128]{2,1,0:T(8,128)(2,1)S(1)} %copy-done.4, ...), custom_call_target="tpu_custom_call" | custom-call | flops 7247757312 | bytes 5505024 | tf_op jit(solution)/shard_map/attend/pallas_call | solution.py:149
  113.8 6.6 %all-to-all-start.2 = ((bf16[16,96,128]{2,1,0:T(8,128)(2,1)}), bf16[16,96,128]{2,1,0:T(8,128)(2,1)S(1)}, u32[]{:S(2)}, u32[]{:S(2)}) async-start(bf16[16,96,128]{2,1,0:T(8,128)(2,1)} %attend.1), calls=%async_computation.2 | async-start | bytes 786432 | tf_op jit(solution)/shard_map/all_to_all | solution.py:241
  121.1 22.6 %all-to-all-done.2.returned_ref = bf16[16,96,128]{2,1,0:T(8,128)(2,1)S(1)} async-done(((bf16[16,96,128]{2,1,0:T(8,128)(2,1)}), bf16[16,96,128]{2,1,0:T(8,128)(2,1)S(1)}, u32[]{:S(2)}, u32[]{:S(2)}) %all-to-all-start.2) | async-done | bytes 393248 | tf_op jit(solution)/shard_map/all_to_all | solution.py:241
  143.8 0.2 update.1
  143.9 0.7 collective-permute-start.6
  144.6 0.7 collective-permute-start.7
  145.3 0.7 collective-permute-start.8
  146.0 8.5 %collective-permute-start.5 = (bf16[1,96,2048]{2,1,0:T(8,128)(2,1)S(1)}, bf16[1,96,2048]{2,1,0:T(8,128)(2,1)S(1)}, u32[]{:S(2)}, u32[]{:S(2)}) collective-permute-start(bf16[1,96,2048]{2,1,0:T(8,128)(2,1)S(1)} %get-tuple-element.11), channel_id=1, source_target_pairs={{0,480},{32,0},{64,32},{96,64},{128,96},{160,128},{192,160},{224,1... | collective-permute-start | bytes 1179656 | tf_op jit(solution)/shard_map/ppermute | solution.py:244
  154.6 0.7 collective-permute-start.11
  155.2 0.7 collective-permute-start.10
  155.9 1.3 collective-permute-start.9
  157.2 4.4 %collective-permute-done.9.refs_0_ = bf16[96,128]{1,0:T(8,128)(2,1)S(1)} collective-permute-done((bf16[96,128]{1,0:T(8,128)(2,1)S(1)}, bf16[96,128]{1,0:T(8,128)(2,1)S(1)}, u32[]{:S(2)}, u32[]{:S(2)}) %collective-permute-start.9) | collective-permute-done | bytes 24608 | tf_op jit(solution)/shard_map/ppermute | solution.py:222
  161.6 0.8 finish.1
  (16 shorter events, 0.1 us)
Async XLA Ops:
  3.5 54.5 %all-to-all-start = ((bf16[16,192,128]{2,1,0:T(8,128)(2,1)}), bf16[16,192,128]{2,1,0:T(8,128)(2,1)S(1)}, u32[]{:S(2)}, u32[]{:S(2)}) async-start(bf16[16,192,128]{2,1,0:T(8,128)(2,1)} %pack.2), calls=%async_computation | async-start | bytes 1572864 | tf_op jit(solution)/shard_map/all_to_all | solution.py:231
  58.0 16.1 %collective-permute-start.3 = (bf16[16,192,128]{2,1,0:T(8,128)(2,1)S(1)}, bf16[16,192,128]{2,1,0:T(8,128)(2,1)S(1)}, u32[]{:S(2)}, u32[]{:S(2)}) collective-permute-start(bf16[16,192,128]{2,1,0:T(8,128)(2,1)S(1)} %all-to-all-done.refs_0_), channel_id=1, source_target_pairs={{32,0},{64,32},{96,64},{128,96},{160,128},{192,160},{224,192},{256... | collective-permute-start | bytes 2359304 | tf_op jit(solution)/shard_map/ppermute | solution.py:21
  60.3 15.8 %collective-permute-start.1 = (bf16[16,192,128]{2,1,0:T(8,128)(2,1)S(1)}, bf16[16,192,128]{2,1,0:T(8,128)(2,1)S(1)}, u32[]{:S(2)}, u32[]{:S(2)}) collective-permute-start(bf16[16,192,128]{2,1,0:T(8,128)(2,1)S(1)} %all-to-all-done.refs_0_), channel_id=1, source_target_pairs={{0,32},{32,64},{64,96},{96,128},{128,160},{160,192},{192,224},{224... | collective-permute-start | bytes 2359304 | tf_op jit(solution)/shard_map/ppermute | solution.py:21
  63.8 30.1 %all-to-all-start.1 = ((bf16[16,96,128]{2,1,0:T(8,128)(2,1)}), bf16[16,96,128]{2,1,0:T(8,128)(2,1)S(1)}, u32[]{:S(2)}, u32[]{:S(2)}) async-start(bf16[16,96,128]{2,1,0:T(8,128)(2,1)} %pack.3), calls=%async_computation.1 | async-start | bytes 786432 | tf_op jit(solution)/shard_map/all_to_all | solution.py:237
  71.1 7.3 %collective-permute-start = (bf16[16,192,128]{2,1,0:T(8,128)(2,1)S(1)}, bf16[16,192,128]{2,1,0:T(8,128)(2,1)S(1)}, u32[]{:S(2)}, u32[]{:S(2)}) collective-permute-start(bf16[16,192,128]{2,1,0:T(8,128)(2,1)S(1)} %all-to-all-done.refs_0_), channel_id=1, source_target_pairs={{0,1},{1,0},{2,3},{3,2},{4,5},{5,4},{6,7},{7,6},{8,9},{9,8},{10,11... | collective-permute-start | bytes 2359304 | tf_op jit(solution)/shard_map/ppermute | solution.py:25
  74.0 19.9 %collective-permute-start.4 = (bf16[16,192,128]{2,1,0:T(8,128)(2,1)S(1)}, bf16[16,192,128]{2,1,0:T(8,128)(2,1)}, u32[]{:S(2)}, u32[]{:S(2)}) collective-permute-start(bf16[16,192,128]{2,1,0:T(8,128)(2,1)S(1)} %collective-permute-done.3.refs_4_), channel_id=1, source_target_pairs={{0,1},{1,0},{2,3},{3,2},{4,5},{5,4},{6,7},{7,6},{8,9},{9,8},{10,11... | collective-permute-start | bytes 2359304 | tf_op jit(solution)/shard_map/ppermute | solution.py:25
  76.1 17.8 %collective-permute-start.2 = (bf16[16,192,128]{2,1,0:T(8,128)(2,1)S(1)}, bf16[16,192,128]{2,1,0:T(8,128)(2,1)}, u32[]{:S(2)}, u32[]{:S(2)}) collective-permute-start(bf16[16,192,128]{2,1,0:T(8,128)(2,1)S(1)} %collective-permute-done.1.refs_2_), channel_id=1, source_target_pairs={{0,1},{1,0},{2,3},{3,2},{4,5},{5,4},{6,7},{7,6},{8,9},{9,8},{10,11... | collective-permute-start | bytes 2359304 | tf_op jit(solution)/shard_map/ppermute | solution.py:25
  78.5 0.9 copy-start.3
  94.0 1.1 copy-start.4
  95.1 48.6 %copy-start.1 = (bf16[1,96,2048]{2,1,0:T(8,128)(2,1)S(1)}, bf16[1,96,2048]{2,1,0:T(8,128)(2,1)}, u32[]{:S(2)}) copy-start(bf16[1,96,2048]{2,1,0:T(8,128)(2,1)} %residual_ref.1) | copy-start | bytes 1179652
  95.1 48.6 %copy-start.2 = (bf16[96,2048]{1,0:T(8,128)(2,1)S(1)}, bf16[96,2048]{1,0:T(8,128)(2,1)}, u32[]{:S(2)}) copy-start(bf16[96,2048]{1,0:T(8,128)(2,1)} %incoming_ref.1) | copy-start | bytes 1179652
  113.8 29.9 %copy-start = (f32[50,2048]{1,0:T(8,128)S(1)}, f32[50,2048]{1,0:T(8,128)}, u32[]{:S(2)}) copy-start(f32[50,2048]{1,0:T(8,128)} %gate_ref.1) | copy-start | bytes 1228804
  113.8 29.9 %all-to-all-start.2 = ((bf16[16,96,128]{2,1,0:T(8,128)(2,1)}), bf16[16,96,128]{2,1,0:T(8,128)(2,1)S(1)}, u32[]{:S(2)}, u32[]{:S(2)}) async-start(bf16[16,96,128]{2,1,0:T(8,128)(2,1)} %attend.1), calls=%async_computation.2 | async-start | bytes 786432 | tf_op jit(solution)/shard_map/all_to_all | solution.py:241
  143.9 10.6 %collective-permute-start.6 = (bf16[4,96,128]{2,1,0:T(8,128)(2,1)S(1)}, bf16[4,96,128]{2,1,0:T(8,128)(2,1)S(1)}, u32[]{:S(2)}, u32[]{:S(2)}) collective-permute-start(bf16[4,96,128]{2,1,0:T(8,128)(2,1)S(1)} %get-tuple-element.13), channel_id=1, source_target_pairs={{0,128},{1,129},{2,130},{3,131},{4,132},{5,133},{6,134},{7,135},{8... | collective-permute-start | bytes 294920 | tf_op jit(solution)/shard_map/ppermute | solution.py:219
  144.6 9.9 %collective-permute-start.7 = (bf16[4,96,128]{2,1,0:T(8,128)(2,1)S(1)}, bf16[4,96,128]{2,1,0:T(8,128)(2,1)S(1)}, u32[]{:S(2)}, u32[]{:S(2)}) collective-permute-start(bf16[4,96,128]{2,1,0:T(8,128)(2,1)S(1)} %get-tuple-element.14), channel_id=1, source_target_pairs={{0,256},{1,257},{2,258},{3,259},{4,260},{5,261},{6,262},{7,263},{8... | collective-permute-start | bytes 294920 | tf_op jit(solution)/shard_map/ppermute | solution.py:219
  145.3 9.2 %collective-permute-start.8 = (bf16[4,96,128]{2,1,0:T(8,128)(2,1)S(1)}, bf16[4,96,128]{2,1,0:T(8,128)(2,1)S(1)}, u32[]{:S(2)}, u32[]{:S(2)}) collective-permute-start(bf16[4,96,128]{2,1,0:T(8,128)(2,1)S(1)} %get-tuple-element.15), channel_id=1, source_target_pairs={{0,384},{1,385},{2,386},{3,387},{4,388},{5,389},{6,390},{7,391},{8... | collective-permute-start | bytes 294920 | tf_op jit(solution)/shard_map/ppermute | solution.py:219
  146.0 15.7 %collective-permute-start.5 = (bf16[1,96,2048]{2,1,0:T(8,128)(2,1)S(1)}, bf16[1,96,2048]{2,1,0:T(8,128)(2,1)S(1)}, u32[]{:S(2)}, u32[]{:S(2)}) collective-permute-start(bf16[1,96,2048]{2,1,0:T(8,128)(2,1)S(1)} %get-tuple-element.11), channel_id=1, source_target_pairs={{0,480},{32,0},{64,32},{96,64},{128,96},{160,128},{192,160},{224,1... | collective-permute-start | bytes 1179656 | tf_op jit(solution)/shard_map/ppermute | solution.py:244
  154.6 2.7 %collective-permute-start.11 = (bf16[96,128]{1,0:T(8,128)(2,1)S(1)}, bf16[96,128]{1,0:T(8,128)(2,1)S(1)}, u32[]{:S(2)}, u32[]{:S(2)}) collective-permute-start(bf16[96,128]{1,0:T(8,128)(2,1)S(1)} %get-tuple-element.16), channel_id=1, source_target_pairs={{0,96},{128,224},{256,352},{384,480},{1,97},{129,225},{257,353},{3... | collective-permute-start | bytes 73736 | tf_op jit(solution)/shard_map/ppermute | solution.py:222
  155.2 2.0 %collective-permute-start.10 = (bf16[96,128]{1,0:T(8,128)(2,1)S(1)}, bf16[96,128]{1,0:T(8,128)(2,1)S(1)}, u32[]{:S(2)}, u32[]{:S(2)}) collective-permute-start(bf16[96,128]{1,0:T(8,128)(2,1)S(1)} %get-tuple-element.17), channel_id=1, source_target_pairs={{0,64},{128,192},{256,320},{384,448},{1,65},{129,193},{257,321},{3... | collective-permute-start | bytes 73736 | tf_op jit(solution)/shard_map/ppermute | solution.py:222
  155.9 5.7 %collective-permute-start.9 = (bf16[96,128]{1,0:T(8,128)(2,1)S(1)}, bf16[96,128]{1,0:T(8,128)(2,1)S(1)}, u32[]{:S(2)}, u32[]{:S(2)}) collective-permute-start(bf16[96,128]{1,0:T(8,128)(2,1)S(1)} %get-tuple-element.18), channel_id=1, source_target_pairs={{0,32},{128,160},{256,288},{384,416},{1,33},{129,161},{257,289},{3... | collective-permute-start | bytes 73736 | tf_op jit(solution)/shard_map/ppermute | solution.py:222
